TPU v7x, 512 devices: a whole 4x4x16 slice. The times are simulated.
512 devices in a mesh: tm: 8 (over x, y_lo), mesh: 64 (over y_hi, z, core).
Axes of the slice: x: 4, y: 4 (y_hi: 2, y_lo: 2; y = y_hi * 2 + y_lo), z: 16, core: 2. Of those that a mesh axis runs over, the one named last changes fastest.
Arguments:
- iterate: float32 [3, 64, 512, 512], P(None, 'tm', 'mesh'), may hold values from -6 to 6
- forcing: float32 [3, 64, 512, 512], P(None, 'tm', 'mesh'), may hold values from -6 to 6
- start_state: float32 [3, 512, 512], P(None, 'mesh'), may hold values from -6 to 6
- damping: float32 [512, 512], P('mesh'), may hold values from 0.4 to 3
- coriolis: float32 [512, 512], P('mesh'), may hold values from -1 to 1
- coupling: float32 [512, 512], P('mesh'), may hold values from 0.04 to 0.12
- edge_order: int32 [64, 2, 512], P('mesh'), may hold values from 0 to 511, each once within a row
Outputs:
- updated: float32 [3, 64, 512, 512], P(None, 'tm', 'mesh')
Inputs may be any that keep to these rules, and one draw needn't show every extreme that they name: edge_order[p,0] and edge_order[p,1] are each a permutation of 0..511.
All inputs are finite; a program needn't handle non-finite values.
Results may differ from a plain program's by a relative error of at most 0.0003.
Values sent between devices are 32-bit elements; how exact they have to be, the bound alone decides.
A program may use at most 64 MiB of HBM per device.

v0:
```python
import math

import jax
import jax.numpy as jnp
from jax import lax
from jax.sharding import PartitionSpec as P

SWEEPS = 4


alpha_corner = 0.1
half_root = math.sqrt(3.0) / 2.0


def passed_along(block, axis, distance):
    devices = range(lax.axis_size(axis))
    route = [(i - distance, i) for i in devices if i - distance in devices]
    return lax.ppermute(block, axis, route)


def with_halo(cells, sides, width):
    for axis, dim in sides:
        count = lax.axis_size(axis)
        head = lax.slice_in_dim(cells, 0, width, axis=dim)
        tail = lax.slice_in_dim(cells, cells.shape[dim] - width, cells.shape[dim], axis=dim)
        cells = jnp.concatenate(
            [
                lax.ppermute(tail, axis, [(i, (i + 1) % count) for i in range(count)]),
                cells,
                lax.ppermute(head, axis, [((i + 1) % count, i) for i in range(count)]),
            ],
            axis=dim,
        )
    return cells


def sample_rows(field):
    middle = field[..., 1:-1, :]
    upper = field[..., 2:, :]
    lower = field[..., :-2, :]
    east = jnp.roll(middle, -1, axis=-1)
    west = jnp.roll(middle, 1, axis=-1)
    north_west = jnp.roll(upper, 1, axis=-1)
    south_east = jnp.roll(lower, -1, axis=-1)
    along_x = east - west + 0.5 * (upper - north_west - lower + south_east)
    along_y = half_root * (upper + north_west - lower - south_east)
    return (along_x, along_y)


def couple(height, east_vel, north_vel, coupling):
    height_x, height_y = sample_rows(height)
    east_x, east_y = sample_rows(east_vel)
    north_x, north_y = sample_rows(north_vel)
    return (coupling * (east_x + north_y), coupling * height_x, coupling * height_y)


def phase_table(rows_idx, cols_idx, total):
    product = rows_idx[:, None] * cols_idx[None, :] % total
    angle = product.astype(jnp.float32) * (2.0 * math.pi / total)
    return (jnp.cos(angle), jnp.sin(angle))


def block_solve(source, lam_re, lam_im, damping, coriolis):
    a_re = lam_re + damping
    a_im = lam_im + 0.0 * damping
    a_abs = a_re * a_re + a_im * a_im
    h_re = (source[0, 0] * a_re + source[1, 0] * a_im) / a_abs
    h_im = (source[1, 0] * a_re - source[0, 0] * a_im) / a_abs
    d_re = a_re * a_re - a_im * a_im + coriolis * coriolis
    d_im = 2.0 * a_re * a_im
    d_abs = d_re * d_re + d_im * d_im
    nu_re = a_re * source[0, 1] - a_im * source[1, 1] + coriolis * source[0, 2]
    nu_im = a_re * source[1, 1] + a_im * source[0, 1] + coriolis * source[1, 2]
    nv_re = a_re * source[0, 2] - a_im * source[1, 2] - coriolis * source[0, 1]
    nv_im = a_re * source[1, 2] + a_im * source[0, 2] - coriolis * source[1, 1]
    u_re = (nu_re * d_re + nu_im * d_im) / d_abs
    u_im = (nu_im * d_re - nu_re * d_im) / d_abs
    v_re = (nv_re * d_re + nv_im * d_im) / d_abs
    v_im = (nv_im * d_re - nv_re * d_im) / d_abs
    return jnp.stack([jnp.stack([h_re, u_re, v_re]), jnp.stack([h_im, u_im, v_im])])


def fix_rims(padded, order):
    below = jnp.take(padded[..., 0, :], order[0], axis=-1)
    above = jnp.take(padded[..., -1, :], order[1], axis=-1)
    return jnp.concatenate(
        [below[..., None, :], padded[..., 1:-1, :], above[..., None, :]], axis=-2
    )


def on_device(iterate, forcing, start_state, damping, coriolis, coupling, edge_order):
    steps = iterate.shape[1]
    groups = lax.axis_size("tm")
    total = steps * groups
    group = lax.axis_index("tm")
    local_times = group * steps + jnp.arange(steps, dtype=jnp.int32)
    timef = local_times.astype(jnp.float32)
    log_alpha = math.log(alpha_corner)
    beta = math.exp(log_alpha / total)
    order = edge_order[0]
    high = lax.Precision.HIGHEST
    carried = passed_along(iterate[:, -1], "tm", 1)
    carried = jnp.where(group == 0, start_state, carried)
    previous = jnp.concatenate([carried[:, None], iterate[:, :-1]], axis=1)
    padded = fix_rims(with_halo(iterate, (("mesh", 2),), 1), order)
    off_h, off_u, off_v = couple(padded[0], padded[1], padded[2], coupling)
    applied = jnp.stack(
        [
            damping * iterate[0] + off_h,
            damping * iterate[1] - coriolis * iterate[2] + off_u,
            damping * iterate[2] + coriolis * iterate[1] + off_v,
        ]
    )
    residual = forcing + previous - iterate - applied
    scaled = residual * jnp.exp(timef * (log_alpha / total))[None, :, None, None]
    piece = lax.all_gather(scaled, "tm", axis=1, tiled=True)
    times = jnp.arange(piece.shape[1], dtype=jnp.int32)
    cos_t, sin_t = phase_table(local_times, times, total)
    part_re = jnp.einsum("kn,cnhw->ckhw", cos_t, piece, precision=high)
    part_im = -jnp.einsum("kn,cnhw->ckhw", sin_t, piece, precision=high)
    spectrum = jnp.stack([part_re, part_im])
    angle = timef * (2.0 * math.pi / total)
    lam_re = (1.0 - beta * jnp.cos(angle))[:, None, None]
    lam_im = (beta * jnp.sin(angle))[:, None, None]
    solved = block_solve(spectrum, lam_re, lam_im, damping, coriolis)
    for sweep in range(SWEEPS - 1):
        rims = fix_rims(with_halo(solved, (("mesh", 3),), 1), order)
        off_h, off_u, off_v = couple(rims[:, 0], rims[:, 1], rims[:, 2], coupling)
        solved = block_solve(
            spectrum - jnp.stack([off_h, off_u, off_v], axis=1), lam_re, lam_im, damping, coriolis
        )
    piece = lax.all_gather(solved, "tm", axis=2, tiled=True)
    freqs = jnp.arange(piece.shape[2], dtype=jnp.int32)
    cos_t, sin_t = phase_table(local_times, freqs, total)
    summed = jnp.einsum("nk,ckhw->cnhw", cos_t, piece[0], precision=high) - jnp.einsum(
        "nk,ckhw->cnhw", sin_t, piece[1], precision=high
    )
    unscale = jnp.exp(-timef * (log_alpha / total)) / total
    return iterate + summed * unscale[None, :, None, None]


def solution(mesh):
    in_specs = (
        P(None, "tm", "mesh", None),
        P(None, "tm", "mesh", None),
        P(None, "mesh", None),
        P("mesh", None),
        P("mesh", None),
        P("mesh", None),
        P("mesh", None, None),
    )
    out_specs = P(None, "tm", "mesh", None)
    return jax.shard_map(
        on_device, mesh=mesh, in_specs=in_specs, out_specs=out_specs, check_vma=False
    )
```

profile of v0, /device:TPU:42, one launch (start us, length us, event | category | flops | bytes accessed | tf_op | source)
XLA Modules:
  0.0 361.4 jit_solution(8948516643057982678)
XLA Ops:
  7.3 3.3 collective-permute-start
  13.8 2.4 collective-permute-start.1
  28.5 83.3 %all-gather.3.cloned.1.call-done = f32[3,64,8,512]{3,1,2,0:T(8,128)} async-done(((f32[3,8,8,512]{3,1,2,0:T(8,128)}), f32[3,64,8,512]{3,1,2,0:T(8,128)}) %all-gather.3.cloned.1.call-update) | async-done | bytes 3145744 | tf_op jit(solution)/shard_map/all_gather | solution.py:116
  111.8 3.8 %fusion.2 = f32[1,3,8,8,512]{4,2,3,1,0:T(8,128)S(1)} fusion(f32[3,64,8,512]{3,1,2,0:T(8,128)} %all-gather.3.cloned.1.call-done, s32[8]{0:T(128)S(1)} %iota_add_fusion), kind=kOutput, calls=%fused_computation.65 | convolution fusion | flops 75602944 | bytes 3538976 | tf_op jit(solution)/shard_map/kn,cnhw->ckhw/dot_general | solution.py:120
  119.9 2.6 collective-permute-start.3
  124.6 5.4 %gather_fusion.3 = f32[512,2,3,8]{3,1,2,0:T(2,128)} fusion(f32[2,3,8,512]{2,0,3,1:T(2,128)} %copy.58, s32[1024]{0:T(1024)S(1)} %pad_clamp_fusion), kind=kCustom, calls=%fused_computation.3.clone | custom fusion | bytes 198656 | tf_op jit(solution)/shard_map/jit(_take)/gather | solution.py:85
  130.0 2.4 copy.59
  134.4 5.4 %gather_fusion.2 = f32[512,2,3,8]{3,1,2,0:T(2,128)} fusion(f32[2,3,8,512]{2,0,3,1:T(2,128)} %copy.56, s32[1024]{0:T(1024)S(1)} %pad_clamp_fusion.1), kind=kCustom, calls=%fused_computation.1.clone | custom fusion | bytes 198656 | tf_op jit(solution)/shard_map/jit(_take)/gather | solution.py:84
  139.8 2.4 copy.57
  144.7 3.3 collective-permute-start.6
  148.0 2.1 collective-permute-start.5
  152.2 5.4 %gather_fusion.5 = f32[512,2,3,8]{3,1,2,0:T(2,128)} fusion(f32[2,3,8,512]{2,0,3,1:T(2,128)} %copy.70, s32[1024]{0:T(1024)S(1)} %pad_clamp_fusion), kind=kCustom, calls=%fused_computation.5.clone | custom fusion | bytes 198656 | tf_op jit(solution)/shard_map/jit(_take)/gather | solution.py:85
  157.6 2.4 copy.71
  162.1 5.4 %gather_fusion.4 = f32[512,2,3,8]{3,1,2,0:T(2,128)} fusion(f32[2,3,8,512]{2,0,3,1:T(2,128)} %copy.68, s32[1024]{0:T(1024)S(1)} %pad_clamp_fusion.1), kind=kCustom, calls=%fused_computation.4.clone | custom fusion | bytes 198656 | tf_op jit(solution)/shard_map/jit(_take)/gather | solution.py:84
  167.5 2.4 copy.69
  172.3 5.8 %collective-permute-start.8 = (f32[2,3,8,1,512]{4,2,3,1,0:T(8,128)S(1)}, f32[2,3,8,1,512]{4,2,3,1,0:T(8,128)S(1)}, u32[]{:S(2)}, u32[]{:S(2)}) collective-permute-start(f32[2,3,8,1,512]{4,2,3,1,0:T(8,128)S(1)} %get-tuple-element.47), channel_id=1, source_target_pairs={{1,0},{2,1},{3,2},{4,3},{5,4},{6,5},{7,6},{8,7},{9,8},{10,9},{11,1... | collective-permute-start | bytes 294920 | tf_op jit(solution)/shard_map/ppermute | solution.py:30
  178.1 2.2 collective-permute-start.7
  182.4 5.4 %gather_fusion.7 = f32[512,2,3,8]{3,1,2,0:T(2,128)} fusion(f32[2,3,8,512]{2,0,3,1:T(2,128)} %copy.82, s32[1024]{0:T(1024)S(1)} %pad_clamp_fusion), kind=kCustom, calls=%fused_computation.7.clone | custom fusion | bytes 198656 | tf_op jit(solution)/shard_map/jit(_take)/gather | solution.py:85
  187.8 2.4 copy.83
  192.3 5.4 %gather_fusion.6 = f32[512,2,3,8]{3,1,2,0:T(2,128)} fusion(f32[2,3,8,512]{2,0,3,1:T(2,128)} %copy.80, s32[1024]{0:T(1024)S(1)} %pad_clamp_fusion.1), kind=kCustom, calls=%fused_computation.6.clone | custom fusion | bytes 198656 | tf_op jit(solution)/shard_map/jit(_take)/gather | solution.py:84
  197.7 2.4 copy.81
  203.5 142.6 %all-gather.5.cloned.1.call-done = f32[2,3,64,8,512]{4,2,3,1,0:T(8,128)} async-done(((f32[2,3,8,8,512]{4,2,3,1,0:T(8,128)}), f32[2,3,64,8,512]{4,2,3,1,0:T(8,128)}) %all-gather.5.cloned.1.call-update) | async-done | bytes 6291472 | tf_op jit(solution)/shard_map/all_gather | solution.py:132
  346.1 3.7 %fusion = f32[3,8,512,8]{2,3,1,0:T(8,128)S(1)} fusion(f32[2,3,64,8,512]{4,2,3,1,0:T(8,128)} %all-gather.5.cloned.1.call-done, s32[8]{0:T(128)S(1)} %iota_add_fusion), kind=kOutput, calls=%fused_computation.9 | convolution fusion | flops 75504640 | bytes 3538976 | tf_op jit(solution)/shard_map/nk,ckhw->cnhw/dot_general | solution.py:135
  349.8 3.8 %fusion.6 = f32[3,8,8,512]{3,1,2,0:T(8,128)S(1)} fusion(f32[3,8,512,8]{2,3,1,0:T(8,128)S(1)} %fusion, f32[2,3,64,8,512]{4,2,3,1,0:T(8,128)} %all-gather.5.cloned.1.call-done, f32[8]{0:T(128)S(1)} %exponential_multiply_fusion, s32[8]{0:T(128)S(1)} %iota_add_fusion, f32[3,8,8,512]{3,2,1,0:T(8,128)S(1)} %copy-done.1), kind=kOutput, calls=%fused_computation.70 | convolution fusion | flops 75799552 | bytes 4325440 | tf_op jit(solution)/shard_map/nk,ckhw->cnhw/dot_general | solution.py:135
  (136 shorter events, 41.5 us)
Async XLA Ops:
  6.5 105.2 %all-gather.3.cloned.1.call-start = ((), (), s32[]{:S(2)}) async-start(), calls=%async_computation | async-start | bytes 3538944 | tf_op jit(solution)/shard_map/all_gather | solution.py:116
  7.3 18.1 %collective-permute-start = (f32[3,8,512]{2,1,0:T(8,128)S(1)}, f32[3,8,512]{2,1,0:T(8,128)S(1)}, u32[]{:S(2)}, u32[]{:S(2)}) collective-permute-start(f32[3,8,512]{2,1,0:T(8,128)S(1)} %slice_bitcast_fusion.51), channel_id=1, source_target_pairs={{0,64},{64,128},{128,192},{192,256},{256,320},{320,384},{384,448},... | collective-permute-start | bytes 147464 | tf_op jit(solution)/shard_map/ppermute | solution.py:18
  11.8 10.1 %collective-permute-start.2 = (f32[3,8,1,512]{3,1,0,2:T(8,128)S(1)}, f32[3,8,1,512]{3,1,0,2:T(8,128)S(1)}, u32[]{:S(2)}, u32[]{:S(2)}) collective-permute-start(f32[3,8,1,512]{3,1,0,2:T(8,128)S(1)} %copy.98), channel_id=1, source_target_pairs={{1,0},{2,1},{3,2},{4,3},{5,4},{6,5},{7,6},{8,7},{9,8},{10,9},{11,1... | collective-permute-start | bytes 147464 | tf_op jit(solution)/shard_map/ppermute | solution.py:30
  13.8 5.4 %collective-permute-start.1 = (f32[3,8,1,512]{3,1,0,2:T(8,128)S(1)}, f32[3,8,1,512]{3,1,0,2:T(8,128)S(1)}, u32[]{:S(2)}, u32[]{:S(2)}) collective-permute-start(f32[3,8,1,512]{3,1,0,2:T(8,128)S(1)} %copy.97), channel_id=1, source_target_pairs={{0,1},{1,2},{2,3},{3,4},{4,5},{5,6},{6,7},{7,8},{8,9},{9,10},{10,1... | collective-permute-start | bytes 147464 | tf_op jit(solution)/shard_map/ppermute | solution.py:28
  24.9 0.8 copy-start.6
  24.9 0.9 copy-start.2
  24.9 0.9 copy-start.3
  25.0 0.8 copy-start.4
  25.9 1.0 copy-start.1
  25.9 1.1 copy-start.5
  28.4 317.7 %all-gather.5.cloned.1.call-start = ((), (), s32[]{:S(2)}) async-start(), calls=%async_computation.1 | async-start | bytes 7077888 | tf_op jit(solution)/shard_map/all_gather | solution.py:132
  111.8 3.8 %copy-start = (f32[3,64,8,512]{3,1,2,0:T(8,128)S(1)}, f32[3,64,8,512]{3,1,2,0:T(8,128)}, u32[]{:S(2)}) copy-start(f32[3,64,8,512]{3,1,2,0:T(8,128)} %all-gather.3.cloned.1.call-done) | copy-start | bytes 9437188
  118.0 4.5 %collective-permute-start.4 = (f32[2,3,8,1,512]{4,2,3,1,0:T(8,128)S(1)}, f32[2,3,8,1,512]{4,2,3,1,0:T(8,128)S(1)}, u32[]{:S(2)}, u32[]{:S(2)}) collective-permute-start(f32[2,3,8,1,512]{4,2,3,1,0:T(8,128)S(1)} %get-tuple-element.51), channel_id=1, source_target_pairs={{1,0},{2,1},{3,2},{4,3},{5,4},{6,5},{7,6},{8,7},{9,8},{10,9},{11,1... | collective-permute-start | bytes 294920 | tf_op jit(solution)/shard_map/ppermute | solution.py:30
  119.9 12.5 %collective-permute-start.3 = (f32[2,3,8,1,512]{4,2,3,1,0:T(8,128)S(1)}, f32[2,3,8,1,512]{4,2,3,1,0:T(8,128)S(1)}, u32[]{:S(2)}, u32[]{:S(2)}) collective-permute-start(f32[2,3,8,1,512]{4,2,3,1,0:T(8,128)S(1)} %get-tuple-element.50), channel_id=1, source_target_pairs={{0,1},{1,2},{2,3},{3,4},{4,5},{5,6},{6,7},{7,8},{8,9},{9,10},{10,1... | collective-permute-start | bytes 294920 | tf_op jit(solution)/shard_map/ppermute | solution.py:28
  144.7 5.5 %collective-permute-start.6 = (f32[2,3,8,1,512]{4,2,3,1,0:T(8,128)S(1)}, f32[2,3,8,1,512]{4,2,3,1,0:T(8,128)S(1)}, u32[]{:S(2)}, u32[]{:S(2)}) collective-permute-start(f32[2,3,8,1,512]{4,2,3,1,0:T(8,128)S(1)} %get-tuple-element.49), channel_id=1, source_target_pairs={{1,0},{2,1},{3,2},{4,3},{5,4},{6,5},{7,6},{8,7},{9,8},{10,9},{11,1... | collective-permute-start | bytes 294920 | tf_op jit(solution)/shard_map/ppermute | solution.py:30
  148.0 12.0 %collective-permute-start.5 = (f32[2,3,8,1,512]{4,2,3,1,0:T(8,128)S(1)}, f32[2,3,8,1,512]{4,2,3,1,0:T(8,128)S(1)}, u32[]{:S(2)}, u32[]{:S(2)}) collective-permute-start(f32[2,3,8,1,512]{4,2,3,1,0:T(8,128)S(1)} %get-tuple-element.48), channel_id=1, source_target_pairs={{0,1},{1,2},{2,3},{3,4},{4,5},{5,6},{6,7},{7,8},{8,9},{9,10},{10,1... | collective-permute-start | bytes 294920 | tf_op jit(solution)/shard_map/ppermute | solution.py:28
  172.3 8.0 %collective-permute-start.8 = (f32[2,3,8,1,512]{4,2,3,1,0:T(8,128)S(1)}, f32[2,3,8,1,512]{4,2,3,1,0:T(8,128)S(1)}, u32[]{:S(2)}, u32[]{:S(2)}) collective-permute-start(f32[2,3,8,1,512]{4,2,3,1,0:T(8,128)S(1)} %get-tuple-element.47), channel_id=1, source_target_pairs={{1,0},{2,1},{3,2},{4,3},{5,4},{6,5},{7,6},{8,7},{9,8},{10,9},{11,1... | collective-permute-start | bytes 294920 | tf_op jit(solution)/shard_map/ppermute | solution.py:30
  178.1 12.1 %collective-permute-start.7 = (f32[2,3,8,1,512]{4,2,3,1,0:T(8,128)S(1)}, f32[2,3,8,1,512]{4,2,3,1,0:T(8,128)S(1)}, u32[]{:S(2)}, u32[]{:S(2)}) collective-permute-start(f32[2,3,8,1,512]{4,2,3,1,0:T(8,128)S(1)} %get-tuple-element.46), channel_id=1, source_target_pairs={{0,1},{1,2},{2,3},{3,4},{4,5},{5,6},{6,7},{7,8},{8,9},{9,10},{10,1... | collective-permute-start | bytes 294920 | tf_op jit(solution)/shard_map/ppermute | solution.py:28
Sparse Core Ops, SparseCore 0:
  28.5 83.2 all-gather.2
  203.6 142.4 all-gather.4
where the time goes:
time: 363 us; the launch traced here: 361 us
  waiting for transfers between devices  226 us (62%)
  local copies, waits for them, and re-layouts  73.9 us (20%)
  starting transfers between devices  25.6 us (7%)
  between operations  14.2 us (4%)
  matrix products  13 us (4%)
  other arithmetic  8.47 us (2%)
    all_gather x1, waiting for transfers between devices, on_device(): piece = lax.all_gather(solved, 'tm', axis=2, tiled=True)  143 us
    all_gather x1, waiting for transfers between devices, on_device(): piece = lax.all_gather(scaled, 'tm', axis=1, tiled=True)  83.3 us
    gather x8, local copies, waits for them, and re-layouts, fix_rims(): below = jnp.take(padded[..., 0, :], order[0], axis=-1)  25.7 us
    gather x8, local copies, waits for them, and re-layouts, fix_rims(): above = jnp.take(padded[..., -1, :], order[1], axis=-1)  25.7 us
    ppermute x4, starting transfers between devices, with_halo(): lax.ppermute(head, axis, [((i + 1) % count, i) for i in range(count)])  12.9 us
    ppermute x4, starting transfers between devices, with_halo(): lax.ppermute(tail, axis, [(i, (i + 1) % count) for i in range(count)])  9.32 us
  transfers between devices with their start and end apart: 11, of which 3 were waited for; matrix products, arithmetic and copies ran while one was open for 11% of the time, Pallas kernels for 0%

commit v1 on v0

v1 whole, which is shorter than its diff:
```python
import functools
import math

import jax
import jax.numpy as jnp
import numpy as np
from jax import lax
from jax.experimental import pallas as pl
from jax.experimental.pallas import tpu as pltpu
from jax.sharding import PartitionSpec as P

MESH = pl.DeviceIdType.MESH
ALPHA = 0.1
HALF_ROOT = math.sqrt(3.0) / 2.0
SWEEPS = 4
G = 8
T = 64
L = 128
Q = 4
C = 3
WIDE = Q * C * L
LO, MID, HI = 0, 5, 15
EXT = 18


def tables():
    n = np.arange(T)
    forward = np.zeros((T, T))
    inverse = np.zeros((T, T))
    lam = np.zeros((2, T))
    beta = math.exp(math.log(ALPHA) / T)
    grow = ALPHA ** (n / T)
    for d in range(G):
        for half in range(2):
            for j in range(4):
                slot = 4 * d + j
                row = d * 8 + half * 4 + j
                if slot == 0:
                    freq, weight, part = 32 * half, 1.0, 0
                else:
                    freq, weight, part = slot, 2.0, half
                angle = 2.0 * math.pi * (freq * n % T) / T
                wave = np.cos(angle) if part == 0 else -np.sin(angle)
                forward[row] = wave * grow
                inverse[:, row] = weight * wave / grow / T
                lam[0, row] = 1.0 - beta * math.cos(2.0 * math.pi * freq / T)
                lam[1, row] = 0.0 if slot == 0 else beta * math.sin(2.0 * math.pi * freq / T)
    lam = np.broadcast_to(lam[:, :, None], (2, T, L))
    return [np.asarray(a, np.float32) for a in (forward, inverse, lam)]


def lanes(q, c):
    return pl.ds((q * C + c) * L, L)


def shift(tiles, step):
    lane = lax.broadcasted_iota(jnp.int32, (8, L), 1)
    turned = [pltpu.roll(t, step % L, axis=1) for t in tiles]
    edge = 0 if step == 1 else L - 1
    return [jnp.where(lane == edge, turned[(q - step) % Q], turned[q]) for q in range(Q)]


def permuted(tiles, order):
    out = []
    for q in range(Q):
        high = order[q] // L
        low = order[q] - high * L
        total = None
        for s in range(Q):
            part = jnp.take_along_axis(tiles[s], low, axis=1, mode="promise_in_bounds")
            total = part if total is None else jnp.where(high == s, part, total)
        out.append(total)
    return out


def couple(row, mid, low, up):
    s = HALF_ROOT
    h, u, v = range(3)
    diff = [[up[c][q] - low[c][q] for q in range(Q)] for c in range(3)]
    east = shift([mid[u][q] + 0.5 * low[u][q] - s * low[v][q] for q in range(Q)], -1)
    west = shift([mid[u][q] + 0.5 * up[u][q] - s * up[v][q] for q in range(Q)], 1)
    off_h = [east[q] - west[q] + 0.5 * diff[u][q] + s * diff[v][q] for q in range(Q)]
    low_m, up_p = shift(low[h], -1), shift(up[h], 1)
    mid_m, mid_p = shift(mid[h], -1), shift(mid[h], 1)
    off_u = [mid_m[q] - mid_p[q] + 0.5 * (diff[h][q] - up_p[q] + low_m[q]) for q in range(Q)]
    off_v = [s * (diff[h][q] + up_p[q] - low_m[q]) for q in range(Q)]
    return off_h, off_u, off_v


def load(ref, row):
    return [[ref[row, :, lanes(q, c)] for q in range(Q)] for c in range(C)]


def store(ref, row, tiles):
    for c in range(C):
        for q in range(Q):
            ref[row, :, lanes(q, c)] = tiles[c][q]


def wide(ref, q, i, row):
    return jnp.broadcast_to(ref[q, i, pl.ds(row, 1), :], (8, L))


def kernel(
    bands,
    it_any, fo_any, st_any, damp_any, cori_any, coup_any, order_any, fwd_ref, inv_ref, lam_ref,
    out_ref,
    it_v, fo_v, out_v, st_v, own_c, own_o, low_c, low_o, high_c, high_o, carry, fixed, first,
    rows_t, halo_lo, halo_hi, coef, spec, cur,
    a_send, a_recv, b_send, b_recv, c_send, c_recv, d_send, d_recv,
    in_sem, side_send, side_recv, a_ss, a_rs, b_ss, b_rs, c_ss, c_rs, d_ss, d_rs,
):
    me = lax.axis_index("tm")
    band = lax.axis_index("mesh")
    below = lax.rem(band + bands - 1, bands)
    above = lax.rem(band + 1, bands)

    def by_lanes(wide_ref, tiled_ref, sems, first, into):
        pairs = [(wide_ref.at[:, :, pl.ds(q * L, L)], tiled_ref.at[q]) for q in range(Q)]
        if not into:
            pairs = [(b, a) for a, b in pairs]
        return [pltpu.make_async_copy(a, b, sems.at[first + q]) for q, (a, b) in enumerate(pairs)]

    fields = by_lanes(it_any, it_v, in_sem, 7, True)
    forces = by_lanes(fo_any, fo_v, in_sem, 11, True)
    loads = [
        pltpu.make_async_copy(st_any, st_v, in_sem.at[2]),
        pltpu.make_async_copy(damp_any, fixed.at[0], in_sem.at[3]),
        pltpu.make_async_copy(cori_any, fixed.at[1], in_sem.at[4]),
        pltpu.make_async_copy(coup_any, fixed.at[2], in_sem.at[5]),
        pltpu.make_async_copy(order_any, own_o, in_sem.at[6]),
    ]
    for one in fields + loads + forces:
        one.start()
    barrier = pltpu.get_barrier_semaphore()
    for k in range(1, G):
        pl.semaphore_signal(barrier, 1, device_id={"tm": lax.rem(me + k, G)}, device_id_type=MESH)
    for p in (below, above):
        pl.semaphore_signal(barrier, 1, device_id={"mesh": p}, device_id_type=MESH)

    def side(index, src, dst, device):
        return pltpu.make_async_remote_copy(
            src_ref=src, dst_ref=dst, send_sem=side_send.at[index], recv_sem=side_recv.at[index],
            device_id=device, device_id_type=MESH,
        )

    def exchange(src, dst, ss, rs):
        return [
            pltpu.make_async_remote_copy(
                src_ref=src.at[lax.rem(me + k, G)], dst_ref=dst.at[me],
                send_sem=ss.at[k], recv_sem=rs.at[k],
                device_id={"tm": lax.rem(me + k, G)}, device_id_type=MESH,
            )
            for k in range(1, G)
        ]

    for one in fields:
        one.wait()
    for r in range(8):
        for c in range(C):
            for q in range(Q):
                rows_t[r + 1, :, lanes(q, c)] = it_v[q, c, pl.ds(r, 8, stride=8), :]
    for one in loads:
        one.wait()
    for q in range(Q):
        for i in range(3):
            own_c[q, i] = fixed[i, :, pl.ds(q * L, L)]
    pl.semaphore_wait(barrier, G + 1)
    to_next = {"tm": lax.rem(me + 1, G)}
    sides = [
        side(0, rows_t.at[1], halo_hi, {"mesh": below}),
        side(1, rows_t.at[8], halo_lo, {"mesh": above}),
        side(2, it_v.at[:, :, pl.ds(56, 8), :], carry, to_next),
        side(3, own_c, high_c, {"mesh": below}),
        side(4, own_c, low_c, {"mesh": above}),
        side(5, own_o, high_o, {"mesh": below}),
        side(6, own_o, low_o, {"mesh": above}),
    ]
    for one in sides:
        one.start()

    def order(ref, which):
        return [jnp.broadcast_to(ref[pl.ds(which, 1), pl.ds(q * L, L)], (8, L)) for q in range(Q)]

    for one in forces:
        one.wait()
    for index in (0, 1, 2):
        sides[index].wait_recv()
    low = [[halo_lo[:, lanes(q, c)] for q in range(Q)] for c in range(C)]
    store(rows_t, 0, [permuted(low[c], order(own_o, 0)) for c in range(C)])
    high = [[halo_hi[:, lanes(q, c)] for q in range(Q)] for c in range(C)]
    store(rows_t, 9, [permuted(high[c], order(own_o, 1)) for c in range(C)])

    for q in range(Q):
        for c in range(C):
            first[q, c] = jnp.where(me == 0, st_v[c, :, pl.ds(q * L, L)], carry[q, c])
    sub = lax.broadcasted_iota(jnp.int32, (8, L), 0)

    def residual_row(r, _):
        mid = load(rows_t, r + 1)
        off = couple(r, mid, load(rows_t, r), load(rows_t, r + 2))
        for q in range(Q):
            damp, cori, coup = [wide(own_c, q, i, r) for i in range(3)]
            h, u, v = mid[0][q], mid[1][q], mid[2][q]
            applied = [damp * h, damp * u - cori * v, damp * v + cori * u]
            target = lax.rem(r - 2 * q + 16, G)
            for c in range(C):
                before = jnp.where(sub == 0, wide(first, q, c, r), pltpu.roll(mid[c][q], 1, axis=0))
                force = fo_v[q, c, pl.ds(r, 8, stride=8), :]
                a_send[target, :, lanes(q, c)] = (
                    force + before - mid[c][q] - (applied[c] + coup * off[c][q])
                )
        return 0

    lax.fori_loop(0, 8, residual_row, 0)
    hop_a = exchange(a_send, a_recv, a_ss, a_rs)
    for one in hop_a:
        one.start()
    a_recv[me] = a_send[me]

    for index in (3, 4, 5, 6):
        sides[index].wait_recv()
    lam_re = lam_ref[0, pl.ds(me * 8, 8), :]
    lam_im = lam_ref[1, pl.ds(me * 8, 8), :]
    sign = jnp.where(sub < 4, -1.0, 1.0)

    def coef_row(ref, offset):
        def body(r, _):
            for q in range(Q):
                damp, cori, coup = [wide(ref, q, i, r) for i in range(3)]
                a_re = lam_re + damp
                a_im = lam_im
                inv = 1.0 / (a_re * a_re + a_im * a_im)
                d_re = a_re * a_re - a_im * a_im + cori * cori
                d_im = 2.0 * a_re * a_im
                d_inv = 1.0 / (d_re * d_re + d_im * d_im)
                six = [
                    a_re * inv,
                    -sign * a_im * inv,
                    (a_re * d_re + a_im * d_im) * d_inv,
                    sign * (a_im * d_re - a_re * d_im) * d_inv,
                    cori * d_re * d_inv,
                    -sign * cori * d_im * d_inv,
                    coup,
                ]
                for i in range(7):
                    coef[r + offset, i, :, pl.ds(q * L, L)] = six[i]
            return 0

        return body

    for ref, start, stop, offset in ((own_c, 0, 8, MID), (low_c, 5, 8, LO - 5), (high_c, 0, 3, HI)):
        lax.fori_loop(start, stop, coef_row(ref, offset), 0)

    for one in hop_a:
        one.wait_recv()
    high_prec = lax.Precision.HIGHEST
    b_send[...] = jnp.dot(
        fwd_ref[...], a_recv[...].reshape(T, WIDE), precision=high_prec, preferred_element_type=jnp.float32
    ).reshape(G, 8, WIDE)
    hop_b = exchange(b_send, b_recv, b_ss, b_rs)
    for one in hop_b:
        one.start()
    b_recv[me] = b_send[me]
    for one in hop_b:
        one.wait_recv()
    for r in range(8):
        for q in range(Q):
            for c in range(C):
                spec[MID + r, :, lanes(q, c)] = b_recv[(r - 2 * q) % G, :, lanes(q, c)]
    rims = [
        side(7, spec.at[pl.ds(MID, 3)], spec.at[pl.ds(HI, 3)], {"mesh": below}),
        side(8, spec.at[pl.ds(MID + 5, 3)], spec.at[pl.ds(LO, 3)], {"mesh": above}),
    ]
    for one in rims:
        one.start()

    def solve(row, x):
        out = [[], [], []]
        for q in range(Q):
            k = [coef[row, i, :, pl.ds(q * L, L)] for i in range(6)]
            xh, xu, xv = x[0][q], x[1][q], x[2][q]
            sh, su, sv = [pltpu.roll(t, 4, axis=0) for t in (xh, xu, xv)]
            out[0].append(k[0] * xh + k[1] * sh)
            out[1].append(k[2] * xu + k[3] * su + (k[4] * xv + k[5] * sv))
            out[2].append(k[2] * xv + k[3] * sv - (k[4] * xu + k[5] * su))
        return out

    def first_row(row, _):
        store(cur.at[0], row, solve(row, load(spec, row)))
        return 0

    def sweep_row(src, dst):
        def body(row, _):
            off = couple(row, load(src, row), load(src, row - 1), load(src, row + 1))
            full = load(spec, row)
            x = [
                [full[c][q] - coef[row, 6, :, pl.ds(q * L, L)] * off[c][q] for q in range(Q)]
                for c in range(C)
            ]
            store(dst, row, solve(row, x))
            return 0

        return body

    lax.fori_loop(MID, MID + 8, first_row, 0)
    for one in rims:
        one.wait_recv()
    lax.fori_loop(LO, LO + 3, first_row, 0)
    lax.fori_loop(HI, HI + 3, first_row, 0)
    for sweep in range(SWEEPS - 1):
        src, dst = cur.at[sweep % 2], cur.at[(sweep + 1) % 2]
        reach = SWEEPS - 2 - sweep
        ghosts = [(MID - 1, LO + 2, own_o, 0), (MID + 8, HI, own_o, 1)]
        if reach:
            ghosts += [(LO + 3, MID, low_o, 1), (HI - 1, MID + 7, high_o, 0)]
        for to, source, ref, which in ghosts:
            tiles = load(src, source)
            store(src, to, [permuted(tiles[c], order(ref, which)) for c in range(C)])
        body = sweep_row(src, dst)
        if reach:
            lax.fori_loop(LO + 3 - reach, LO + 3, body, 0)
        lax.fori_loop(MID, MID + 8, body, 0)
        if reach:
            lax.fori_loop(HI, HI + reach, body, 0)

    last = cur.at[(SWEEPS - 1) % 2]
    for r in range(8):
        for q in range(Q):
            for c in range(C):
                c_send[(r - 2 * q) % G, :, lanes(q, c)] = last[MID + r, :, lanes(q, c)]
    hop_c = exchange(c_send, c_recv, c_ss, c_rs)
    for one in hop_c:
        one.start()
    c_recv[me] = c_send[me]
    for one in hop_c:
        one.wait_recv()
    d_send[...] = jnp.dot(
        inv_ref[...], c_recv[...].reshape(T, WIDE), precision=high_prec, preferred_element_type=jnp.float32
    ).reshape(G, 8, WIDE)
    hop_d = exchange(d_send, d_recv, d_ss, d_rs)
    for one in hop_d:
        one.start()
    d_recv[me] = d_send[me]
    for one in hop_d:
        one.wait_recv()
    for r in range(8):
        for q in range(Q):
            for c in range(C):
                out_v[q, c, pl.ds(r, 8, stride=8), :] = (
                    rows_t[r + 1, :, lanes(q, c)] + d_recv[(r - 2 * q) % G, :, lanes(q, c)]
                )
    outs = by_lanes(out_ref, out_v, in_sem, 7, False)
    for one in outs:
        one.start()
    for one in outs:
        one.wait()
    for one in sides + rims + hop_a + hop_b + hop_c + hop_d:
        one.wait_send()


def on_device(bands, iterate, forcing, start_state, damping, coriolis, coupling, edge_order):
    forward, inverse, lam = tables()
    flat = (C, T, Q * L)
    hbm, vmem = pl.BlockSpec(memory_space=pl.ANY), pl.BlockSpec(memory_space=pltpu.VMEM)
    f32, i32 = jnp.float32, jnp.int32
    block = pltpu.VMEM((G, 8, WIDE), f32)
    staged = pltpu.VMEM((3, 8, Q * L), f32)
    own, pair = pltpu.VMEM((Q, 3, 8, L), f32), pltpu.VMEM((2, Q * L), i32)
    tiled = pltpu.VMEM((Q, C, T, L), f32)
    row = pltpu.VMEM((8, WIDE), f32)
    hops = pltpu.SemaphoreType.DMA((G,))
    out = pl.pallas_call(
        functools.partial(kernel, bands),
        out_shape=jax.ShapeDtypeStruct(flat, f32),
        in_specs=[hbm] * 7 + [vmem] * 3,
        out_specs=hbm,
        scratch_shapes=[
            tiled, tiled, tiled, staged, own, pair, own, pair, own, pair, own, staged, own,
            pltpu.VMEM((10, 8, WIDE), f32), row, row,
            pltpu.VMEM((EXT, 7, 8, Q * L), f32),
            pltpu.VMEM((EXT, 8, WIDE), f32),
            pltpu.VMEM((2, EXT, 8, WIDE), f32),
        ]
        + [block] * 8
        + [pltpu.SemaphoreType.DMA((15,)), pltpu.SemaphoreType.DMA((9,)), pltpu.SemaphoreType.DMA((9,))]
        + [hops] * 8,
        compiler_params=pltpu.CompilerParams(
            collective_id=0, has_side_effects=True, vmem_limit_bytes=32 * 1024 * 1024
        ),
    )(
        iterate.reshape(flat), forcing.reshape(flat), start_state, damping, coriolis, coupling,
        edge_order.reshape(2, Q * L), forward, inverse, lam,
    )
    return out.reshape(iterate.shape)


def solution(mesh):
    in_specs = (
        P(None, "tm", "mesh", None),
        P(None, "tm", "mesh", None),
        P(None, "mesh", None),
        P("mesh", None),
        P("mesh", None),
        P("mesh", None),
        P("mesh", None, None),
    )
    return jax.shard_map(
        functools.partial(on_device, mesh.shape["mesh"]),
        mesh=mesh, in_specs=in_specs, out_specs=P(None, "tm", "mesh", None), check_vma=False,
    )
```

time: 363 us -> 64.8 us (0.18)
  the two profiles are of different devices: /device:TPU:42 before, /device:TPU:8 now
where the time goes in v1:
time: 64.8 us; the launch traced here: 64.2 us
  Pallas kernels  55.4 us (85%)
  local copies, waits for them, and re-layouts  8.73 us (13%)
    pallas_call x1, Pallas kernels, on_device(): pl.pallas_call(functools.partial(kernel, bands), out_shape=jax.ShapeDtype...  55.4 us
    unnamed x21, local copies, waits for them, and re-layouts  8.73 us

profile of v1, /device:TPU:8, one launch (start us, length us, event | category | flops | bytes accessed | tf_op | source)
XLA Modules:
  0.0 64.2 jit_solution(3630897035508162410)
XLA Ops:
  0.0 0.0 copy-start.9
  0.0 0.7 %copy-done.9 = s32[1,2,512]{2,1,0:T(2,128)S(1)} copy-done((s32[1,2,512]{2,1,0:T(2,128)S(1)}, s32[1,2,512]{2,1,0:T(2,128)}, u32[]{:S(2)}) %copy-start.9) | copy-done | bytes 4120
  0.7 0.0 copy-start
  0.7 1.0 %copy-done = f32[3,8,8,512]{3,2,1,0:T(8,128)S(1)} copy-done((f32[3,8,8,512]{3,2,1,0:T(8,128)S(1)}, f32[3,8,8,512]{3,2,1,0:T(8,128)}, u32[]{:S(2)}) %copy-start) | copy-done | bytes 393240
  1.7 0.0 copy-start.1
  1.7 1.0 %copy-done.1 = f32[3,8,8,512]{3,2,1,0:T(8,128)S(1)} copy-done((f32[3,8,8,512]{3,2,1,0:T(8,128)S(1)}, f32[3,8,8,512]{3,2,1,0:T(8,128)}, u32[]{:S(2)}) %copy-start.1) | copy-done | bytes 393240
  2.7 0.0 copy-start.2
  2.7 0.8 %copy-done.2 = f32[2,64,128]{2,1,0:T(8,128)S(1)} copy-done((f32[2,64,128]{2,1,0:T(8,128)S(1)}, f32[2,64,128]{2,1,0:T(8,128)}, u32[]{:S(2)}) %copy-start.2) | copy-done | bytes 65560
  3.5 0.0 copy-start.3
  3.5 0.8 %copy-done.3 = f32[3,8,512]{2,1,0:T(8,128)S(1)} copy-done((f32[3,8,512]{2,1,0:T(8,128)S(1)}, f32[3,8,512]{2,1,0:T(8,128)}, u32[]{:S(2)}) %copy-start.3) | copy-done | bytes 49176
  4.3 0.0 copy-start.4
  4.3 0.8 %copy-done.4 = f32[64,64]{1,0:T(8,128)S(1)} copy-done((f32[64,64]{1,0:T(8,128)S(1)}, f32[64,64]{1,0:T(8,128)}, u32[]{:S(2)}) %copy-start.4) | copy-done | bytes 16408
  5.1 0.0 copy-start.5
  5.1 0.8 %copy-done.5 = f32[64,64]{1,0:T(8,128)S(1)} copy-done((f32[64,64]{1,0:T(8,128)S(1)}, f32[64,64]{1,0:T(8,128)}, u32[]{:S(2)}) %copy-start.5) | copy-done | bytes 16408
  5.8 0.0 copy-start.6
  5.8 0.7 %copy-done.6 = f32[8,512]{1,0:T(8,128)S(1)} copy-done((f32[8,512]{1,0:T(8,128)S(1)}, f32[8,512]{1,0:T(8,128)}, u32[]{:S(2)}) %copy-start.6) | copy-done | bytes 16408
  6.6 0.0 copy-start.7
  6.6 0.7 %copy-done.7 = f32[8,512]{1,0:T(8,128)S(1)} copy-done((f32[8,512]{1,0:T(8,128)S(1)}, f32[8,512]{1,0:T(8,128)}, u32[]{:S(2)}) %copy-start.7) | copy-done | bytes 16408
  7.3 0.0 copy-start.8
  7.3 0.7 %copy-done.8 = f32[8,512]{1,0:T(8,128)S(1)} copy-done((f32[8,512]{1,0:T(8,128)S(1)}, f32[8,512]{1,0:T(8,128)}, u32[]{:S(2)}) %copy-start.8) | copy-done | bytes 16408
  8.0 55.4 %shard_map.100 = f32[3,64,512]{2,1,0:T(8,128)S(1)} custom-call(f32[3,64,512]{2,1,0:T(8,128)S(1)} %bitcast.5, f32[3,64,512]{2,1,0:T(8,128)S(1)} %bitcast.6, f32[3,8,512]{2,1,0:T(8,128)S(1)} %copy-done.3, f32[8,512]{1,0:T(8,128)S(1)} %copy-done.6, f32[8,512]{1,0:T(8,128)S(1)} %copy-done.7, f32[8,512]{1,0:T(8,128)S(1)} %copy-done.8, s32[2,512]{1,0:T(2,128)S(1)} %bitcast.7, ...), custom_call_target="tpu_custom_call" | custom-call | tf_op jit(solution)/shard_map/pallas_call | solution.py:373
  63.4 0.7 %copy.12 = f32[3,8,8,512]{3,2,1,0:T(8,128)} copy(f32[3,8,8,512]{3,2,1,0:T(8,128)S(1)} %bitcast.4) | data formatting | bytes 786432
Async XLA Ops:
  0.0 0.7 %copy-start.9 = (s32[1,2,512]{2,1,0:T(2,128)S(1)}, s32[1,2,512]{2,1,0:T(2,128)}, u32[]{:S(2)}) copy-start(s32[1,2,512]{2,1,0:T(2,128)} %param.16) | copy-start | bytes 12292
  0.7 1.0 %copy-start = (f32[3,8,8,512]{3,2,1,0:T(8,128)S(1)}, f32[3,8,8,512]{3,2,1,0:T(8,128)}, u32[]{:S(2)}) copy-start(f32[3,8,8,512]{3,2,1,0:T(8,128)} %param.10) | copy-start | bytes 1179652
  1.7 1.0 %copy-start.1 = (f32[3,8,8,512]{3,2,1,0:T(8,128)S(1)}, f32[3,8,8,512]{3,2,1,0:T(8,128)}, u32[]{:S(2)}) copy-start(f32[3,8,8,512]{3,2,1,0:T(8,128)} %param.11) | copy-start | bytes 1179652
  2.7 0.8 %copy-start.2 = (f32[2,64,128]{2,1,0:T(8,128)S(1)}, f32[2,64,128]{2,1,0:T(8,128)}, u32[]{:S(2)}) copy-start(f32[2,64,128]{2,1,0:T(8,128)} %constant.8.clone.lam_ref) | copy-start | bytes 196612
  3.5 0.8 %copy-start.3 = (f32[3,8,512]{2,1,0:T(8,128)S(1)}, f32[3,8,512]{2,1,0:T(8,128)}, u32[]{:S(2)}) copy-start(f32[3,8,512]{2,1,0:T(8,128)} %st_any.1) | copy-start | bytes 147460
  4.3 0.8 %copy-start.4 = (f32[64,64]{1,0:T(8,128)S(1)}, f32[64,64]{1,0:T(8,128)}, u32[]{:S(2)}) copy-start(f32[64,64]{1,0:T(8,128)} %constant.7.clone.inv_ref) | copy-start | bytes 49156
  5.1 0.8 %copy-start.5 = (f32[64,64]{1,0:T(8,128)S(1)}, f32[64,64]{1,0:T(8,128)}, u32[]{:S(2)}) copy-start(f32[64,64]{1,0:T(8,128)} %constant.6.clone.fwd_ref) | copy-start | bytes 49156
  5.8 0.7 %copy-start.6 = (f32[8,512]{1,0:T(8,128)S(1)}, f32[8,512]{1,0:T(8,128)}, u32[]{:S(2)}) copy-start(f32[8,512]{1,0:T(8,128)} %damp_any.1) | copy-start | bytes 49156
  6.6 0.7 %copy-start.7 = (f32[8,512]{1,0:T(8,128)S(1)}, f32[8,512]{1,0:T(8,128)}, u32[]{:S(2)}) copy-start(f32[8,512]{1,0:T(8,128)} %cori_any.1) | copy-start | bytes 49156
  7.3 0.7 %copy-start.8 = (f32[8,512]{1,0:T(8,128)S(1)}, f32[8,512]{1,0:T(8,128)}, u32[]{:S(2)}) copy-start(f32[8,512]{1,0:T(8,128)} %coup_any.1) | copy-start | bytes 49156

commit v2 on v1

v2 whole, which is shorter than its diff:
```python
import functools
import math

import jax
import jax.numpy as jnp
import numpy as np
from jax import lax
from jax.experimental import pallas as pl
from jax.experimental.pallas import tpu as pltpu
from jax.sharding import PartitionSpec as P

MESH = pl.DeviceIdType.MESH
ALPHA = 0.1
HALF_ROOT = math.sqrt(3.0) / 2.0
SWEEPS = 4
G = 8
T = 64
L = 128
Q = 4
C = 3
WIDE = Q * C * L
BLOCK = C * L
LO, MID, HI = 0, 5, 15
EXT = 18
FORTH = ((0, 3), (3, 1))
BACK = ((0, 1), (1, 2), (3, 1))
FAR = ((2, 1), (2, 0), (1, 1), (3, 1), (1, 0), (3, 0), (0, 1))


def tables():
    n = np.arange(T)
    forward = np.zeros((T, T))
    inverse = np.zeros((T, T))
    lam = np.zeros((2, T))
    beta = math.exp(math.log(ALPHA) / T)
    grow = ALPHA ** (n / T)
    for d in range(G):
        for half in range(2):
            for j in range(4):
                slot = 4 * d + j
                row = d * 8 + half * 4 + j
                if slot == 0:
                    freq, weight, part = 32 * half, 1.0, 0
                else:
                    freq, weight, part = slot, 2.0, half
                angle = 2.0 * math.pi * (freq * n % T) / T
                wave = np.cos(angle) if part == 0 else -np.sin(angle)
                forward[row] = wave * grow
                inverse[:, row] = weight * wave / grow / T
                lam[0, row] = 1.0 - beta * math.cos(2.0 * math.pi * freq / T)
                lam[1, row] = 0.0 if slot == 0 else beta * math.sin(2.0 * math.pi * freq / T)
    later = np.concatenate([forward[:, 8::8], np.zeros((T, 1))], axis=1)
    forward = np.concatenate([forward, later], axis=1)
    lam = np.broadcast_to(lam[:, :, None], (2, T, L))
    return [np.asarray(a, np.float32) for a in (forward, inverse, lam)]


def lanes(q, c):
    return pl.ds((q * C + c) * L, L)


def shift(tiles, step):
    lane = lax.broadcasted_iota(jnp.int32, (8, L), 1)
    turned = [pltpu.roll(t, step % L, axis=1) for t in tiles]
    edge = 0 if step == 1 else L - 1
    return [jnp.where(lane == edge, turned[(q - step) % Q], turned[q]) for q in range(Q)]


def permuted(tiles, order):
    out = []
    for q in range(Q):
        high = order[q] // L
        low = order[q] - high * L
        total = None
        for s in range(Q):
            part = jnp.take_along_axis(tiles[s], low, axis=1, mode="promise_in_bounds")
            total = part if total is None else jnp.where(high == s, part, total)
        out.append(total)
    return out


def couple(row, mid, low, up):
    s = HALF_ROOT
    h, u, v = range(3)
    diff = [[up[c][q] - low[c][q] for q in range(Q)] for c in range(3)]
    east = shift([mid[u][q] + 0.5 * low[u][q] - s * low[v][q] for q in range(Q)], -1)
    west = shift([mid[u][q] + 0.5 * up[u][q] - s * up[v][q] for q in range(Q)], 1)
    off_h = [east[q] - west[q] + 0.5 * diff[u][q] + s * diff[v][q] for q in range(Q)]
    low_m, up_p = shift(low[h], -1), shift(up[h], 1)
    mid_m, mid_p = shift(mid[h], -1), shift(mid[h], 1)
    off_u = [mid_m[q] - mid_p[q] + 0.5 * (diff[h][q] - up_p[q] + low_m[q]) for q in range(Q)]
    off_v = [s * (diff[h][q] + up_p[q] - low_m[q]) for q in range(Q)]
    return off_h, off_u, off_v


def load(ref, row):
    return [[ref[row, :, lanes(q, c)] for q in range(Q)] for c in range(C)]


def store(ref, row, tiles):
    for c in range(C):
        for q in range(Q):
            ref[row, :, lanes(q, c)] = tiles[c][q]


def wide(ref, q, i, row):
    return jnp.broadcast_to(ref[q, i, pl.ds(row, 1), :], (8, L))


def kernel(
    bands,
    it_any, fo_any, st_any, damp_any, cori_any, coup_any, order_any, fwd_any, inv_any, lam_any,
    out_ref,
    fwd_ref, inv_ref, lam_ref, it_v, fo_v, out_v, st_v, fixed,
    own_c, own_o, low_c, low_o, high_c, high_o, first,
    rows_t, halo_lo, halo_hi, coef, spec, cur,
    e_recv, a_send, a_recv, b_send, b_recv, c_send, c_recv, d_send, d_recv,
    in_sem, side_send, side_recv, e_ss, e_rs, a_ss, a_rs, b_ss, b_rs, c_ss, c_rs, d_ss, d_rs,
):
    me = lax.axis_index("tm")
    me_x, me_y = me // 2, lax.rem(me, 2)
    band = lax.axis_index("mesh")
    below = lax.rem(band + bands - 1, bands)
    above = lax.rem(band + 1, bands)
    peers = [lax.rem(me_x + dx, 4) * 2 + lax.rem(me_y + dy, 2) for dx, dy in FAR]

    def by_lanes(wide_ref, tiled_ref, base, into):
        pairs = [(wide_ref.at[:, :, pl.ds(q * L, L)], tiled_ref.at[q]) for q in range(Q)]
        if not into:
            pairs = [(b, a) for a, b in pairs]
        return [pltpu.make_async_copy(a, b, in_sem.at[base + q]) for q, (a, b) in enumerate(pairs)]

    fields = by_lanes(it_any, it_v, 0, True)
    forces = by_lanes(fo_any, fo_v, 4, True)
    loads = [
        pltpu.make_async_copy(source, target, in_sem.at[8 + i])
        for i, (source, target) in enumerate(
            [
                (st_any, st_v), (damp_any, fixed.at[0]), (cori_any, fixed.at[1]), (coup_any, fixed.at[2]),
                (order_any, own_o), (fwd_any, fwd_ref), (inv_any, inv_ref), (lam_any, lam_ref),
            ]
        )
    ]
    for one in fields + forces + loads:
        one.start()
    barrier = pltpu.get_barrier_semaphore()
    for peer in peers:
        pl.semaphore_signal(barrier, 1, device_id={"tm": peer}, device_id_type=MESH)
    for p in (below, above):
        pl.semaphore_signal(barrier, 1, device_id={"mesh": p}, device_id_type=MESH)

    sent = []

    def remote(src, dst, ss, rs, device):
        one = pltpu.make_async_remote_copy(
            src_ref=src, dst_ref=dst, send_sem=ss, recv_sem=rs, device_id=device, device_id_type=MESH
        )
        sent.append(one)
        return one

    def side(index, src, dst, p):
        return remote(src, dst, side_send.at[index], side_recv.at[index], {"mesh": p})

    def hop(src, dst, ss, rs, groups, index):
        start, count = groups[index]
        part = pl.ds(start, count)
        return [
            remote(
                src.at[peer, part], dst.at[me, part],
                ss.at[index * 7 + k], rs.at[index * 7 + k], {"tm": peer},
            )
            for k, peer in enumerate(peers)
        ]

    def start(copies):
        for one in copies:
            one.start()

    def arrive(copies):
        for one in copies:
            one.wait_recv()

    def keep(src, dst, group):
        for m in range(group[0], group[0] + group[1]):
            dst[me, m] = src[me, m]

    for one in fields:
        one.wait()
    for r in range(8):
        for c in range(C):
            for q in range(Q):
                rows_t[r + 1, :, lanes(q, c)] = it_v[q, c, pl.ds(r, 8, stride=8), :]
    for one in loads + forces:
        one.wait()
    for q in range(Q):
        for i in range(3):
            own_c[q, i] = fixed[i, :, pl.ds(q * L, L)]
            first[q, i] = jnp.where(me == 0, st_v[i, :, pl.ds(q * L, L)], 0.0)

    sub = lax.broadcasted_iota(jnp.int32, (8, L), 0)

    def residual_row(r, half, m):
        mid = load(rows_t, r + 1)
        off = couple(r, mid, load(rows_t, r), load(rows_t, r + 2))
        for q in range(Q):
            damp, cori, coup = [wide(own_c, q, i, r) for i in range(3)]
            h, u, v = mid[0][q], mid[1][q], mid[2][q]
            applied = [damp * h, damp * u - cori * v, damp * v + cori * u]
            for c in range(C):
                before = jnp.where(sub == 0, wide(first, q, c, r), pltpu.roll(mid[c][q], 1, axis=0))
                force = fo_v[q, c, pl.ds(r, 8, stride=8), :]
                a_send[2 * q + half, m, :, pl.ds(c * L, L)] = (
                    force + before - mid[c][q] - (applied[c] + coup * off[c][q])
                )

    def residual_pair(m, _):
        residual_row(3 - m, 0, m)
        residual_row(4 + m, 1, m)
        return 0

    lax.fori_loop(0, 3, residual_pair, 0)

    pl.semaphore_wait(barrier, 9)
    halos = [side(0, rows_t.at[1], halo_hi, below), side(1, rows_t.at[8], halo_lo, above)]
    start(halos)
    last = pl.ds(T - 8, 8)
    hop_e = [
        remote(it_v.at[peer // 2, :, last, :], e_recv.at[me], e_ss.at[k], e_rs.at[k], {"tm": peer})
        for k, peer in enumerate(peers)
    ]
    start(hop_e)
    hop_a = [hop(a_send, a_recv, a_ss, a_rs, FORTH, i) for i in range(len(FORTH))]
    start(hop_a[0])
    params = [
        side(2, own_c, high_c, below), side(3, own_c, low_c, above),
        side(4, own_o, high_o, below), side(5, own_o, low_o, above),
    ]
    start(params)
    e_recv[me] = it_v[me_x, :, last, :]
    keep(a_send, a_recv, FORTH[0])

    def order(ref, which):
        return [jnp.broadcast_to(ref[pl.ds(which, 1), pl.ds(q * L, L)], (8, L)) for q in range(Q)]

    def halo(ref, row, which):
        tiles = [[ref[:, lanes(q, c)] for q in range(Q)] for c in range(C)]
        store(rows_t, row, [permuted(tiles[c], order(own_o, which)) for c in range(C)])

    arrive(halos)
    halo(halo_lo, 0, 0)
    halo(halo_hi, 9, 1)
    residual_pair(3, 0)
    start(hop_a[1])
    keep(a_send, a_recv, FORTH[1])

    lam_re = lam_ref[0, pl.ds(me * 8, 8), :]
    lam_im = lam_ref[1, pl.ds(me * 8, 8), :]
    sign = jnp.where(sub < 4, -1.0, 1.0)

    def coef_row(ref, offset):
        def body(r, _):
            for q in range(Q):
                damp, cori, coup = [wide(ref, q, i, r) for i in range(3)]
                a_re = lam_re + damp
                a_im = lam_im
                inv = 1.0 / (a_re * a_re + a_im * a_im)
                d_re = a_re * a_re - a_im * a_im + cori * cori
                d_im = 2.0 * a_re * a_im
                d_inv = 1.0 / (d_re * d_re + d_im * d_im)
                seven = [
                    a_re * inv,
                    -sign * a_im * inv,
                    (a_re * d_re + a_im * d_im) * d_inv,
                    sign * (a_im * d_re - a_re * d_im) * d_inv,
                    cori * d_re * d_inv,
                    -sign * cori * d_im * d_inv,
                    coup,
                ]
                for i in range(7):
                    coef[r + offset, i, :, pl.ds(q * L, L)] = seven[i]
            return 0

        return body

    lax.fori_loop(0, 8, coef_row(own_c, MID), 0)

    def transform(table, src, dst, m, extra):
        rows = src[:, m].reshape(T, BLOCK)
        if extra is not None:
            rows = jnp.concatenate([rows, extra], axis=0)
        dst[:, m] = jnp.dot(
            table, rows, precision=lax.Precision.HIGHEST, preferred_element_type=jnp.float32
        ).reshape(G, 8, BLOCK)

    def previous(m):
        row = 3 - m + me_y * (1 + 2 * m)
        return jnp.concatenate([e_flat(c, row) for c in range(C)], axis=1)

    def e_flat(c, row):
        return e_recv.reshape(G * C * 8, L)[pl.ds(c * 8 + row, G, stride=C * 8), :]

    arrive(hop_e)
    hop_b = [hop(b_send, b_recv, b_ss, b_rs, FORTH, i) for i in range(len(FORTH))]
    for i, (begin, count) in enumerate(FORTH):
        arrive(hop_a[i])
        for m in range(begin, begin + count):
            transform(fwd_ref[...], a_recv, b_send, m, previous(m))
        start(hop_b[i])
        keep(b_send, b_recv, FORTH[i])

    arrive(params)
    lax.fori_loop(5, 8, coef_row(low_c, LO - 5), 0)
    lax.fori_loop(0, 3, coef_row(high_c, HI), 0)

    def solve(row, x):
        out = [[], [], []]
        for q in range(Q):
            k = [coef[row, i, :, pl.ds(q * L, L)] for i in range(6)]
            xh, xu, xv = x[0][q], x[1][q], x[2][q]
            sh, su, sv = [pltpu.roll(t, 4, axis=0) for t in (xh, xu, xv)]
            out[0].append(k[0] * xh + k[1] * sh)
            out[1].append(k[2] * xu + k[3] * su + (k[4] * xv + k[5] * sv))
            out[2].append(k[2] * xv + k[3] * sv - (k[4] * xu + k[5] * su))
        return out

    def first_row(row):
        store(cur.at[0], row, solve(row, load(spec, row)))

    def sweep_row(level, row):
        src = cur.at[level]
        off = couple(row, load(src, row), load(src, row - 1), load(src, row + 1))
        full = load(spec, row)
        x = [
            [full[c][q] - coef[row, 6, :, pl.ds(q * L, L)] * off[c][q] for q in range(Q)]
            for c in range(C)
        ]
        return solve(row, x)

    def sweep_pair(level, low, high):
        def body(i, _):
            store(cur.at[level + 1], low + i, sweep_row(level, low + i))
            store(cur.at[level + 1], high - i, sweep_row(level, high - i))
            return 0

        return body

    def ghost(level, to, source, ref, which):
        src = cur.at[level]
        tiles = load(src, source)
        store(src, to, [permuted(tiles[c], order(ref, which)) for c in range(C)])

    def own_rows(m, _):
        for half, r in ((0, 3 - m), (1, 4 + m)):
            for q in range(Q):
                for c in range(C):
                    spec[MID + r, :, lanes(q, c)] = b_recv[2 * q + half, m, :, pl.ds(c * L, L)]
        return 0

    def own_first(m, _):
        first_row(MID + 3 - m)
        first_row(MID + 4 + m)
        return 0

    def rim(index, src, dst, count, p):
        return side(index, spec.at[pl.ds(src, count)], spec.at[pl.ds(dst, count)], p)

    rims = [
        rim(6, MID + 1, HI + 1, 2, below), rim(7, MID + 5, LO, 2, above),
        rim(8, MID, HI, 1, below), rim(9, MID + 7, LO + 2, 1, above),
    ]
    arrive(hop_b[0])
    lax.fori_loop(0, 3, own_rows, 0)
    start(rims[:2])
    lax.fori_loop(0, 3, own_first, 0)
    lax.fori_loop(0, 2, sweep_pair(0, MID + 2, MID + 5), 0)
    arrive(hop_b[1])
    own_rows(3, 0)
    start(rims[2:])
    own_first(3, 0)
    ghost(0, LO + 3, MID, low_o, 1)
    ghost(0, HI - 1, MID + 7, high_o, 0)
    lax.fori_loop(0, 1, sweep_pair(0, MID + 1, MID + 6), 0)
    lax.fori_loop(0, 2, sweep_pair(1, MID + 2, MID + 5), 0)

    hop_c = [hop(c_send, c_recv, c_ss, c_rs, BACK, i) for i in range(len(BACK))]

    def last_pair(m):
        for half, r in ((0, 3 - m), (1, 4 + m)):
            tiles = sweep_row(2, MID + r)
            for q in range(Q):
                for c in range(C):
                    c_send[2 * q + half, m, :, pl.ds(c * L, L)] = tiles[c][q]

    def finish(i):
        begin, count = BACK[i]
        if count == 1:
            last_pair(begin)
        else:
            def body(m, _):
                last_pair(m)
                return 0

            lax.fori_loop(begin, begin + count, body, 0)
        start(hop_c[i])
        keep(c_send, c_recv, BACK[i])

    finish(0)
    arrive(rims)

    def rim_first(i, _):
        first_row(LO + i)
        first_row(HI + 2 - i)
        return 0

    lax.fori_loop(0, 3, rim_first, 0)
    ghost(0, MID - 1, LO + 2, own_o, 0)
    ghost(0, MID + 8, HI, own_o, 1)
    lax.fori_loop(0, 2, sweep_pair(0, LO + 1, HI + 1), 0)
    lax.fori_loop(0, 1, sweep_pair(0, MID, MID + 7), 0)
    ghost(1, LO + 3, MID, low_o, 1)
    ghost(1, HI - 1, MID + 7, high_o, 0)
    ghost(1, MID - 1, LO + 2, own_o, 0)
    ghost(1, MID + 8, HI, own_o, 1)
    lax.fori_loop(0, 1, sweep_pair(1, LO + 2, HI), 0)
    lax.fori_loop(0, 2, sweep_pair(1, MID, MID + 7), 0)
    ghost(2, MID - 1, LO + 2, own_o, 0)
    ghost(2, MID + 8, HI, own_o, 1)
    for i in range(1, len(BACK)):
        finish(i)

    hop_d = [hop(d_send, d_recv, d_ss, d_rs, BACK, i) for i in range(len(BACK))]
    for i, (begin, count) in enumerate(BACK):
        arrive(hop_c[i])
        for m in range(begin, begin + count):
            transform(inv_ref[...], c_recv, d_send, m, None)
        start(hop_d[i])
        keep(d_send, d_recv, BACK[i])
    for i, (begin, count) in enumerate(BACK):
        arrive(hop_d[i])
        for m in range(begin, begin + count):
            for half, r in ((0, 3 - m), (1, 4 + m)):
                for q in range(Q):
                    for c in range(C):
                        out_v[q, c, pl.ds(r, 8, stride=8), :] = (
                            rows_t[r + 1, :, lanes(q, c)] + d_recv[2 * q + half, m, :, pl.ds(c * L, L)]
                        )
    outs = by_lanes(out_ref, out_v, 0, False)
    for one in outs:
        one.start()
    for one in outs:
        one.wait()
    for one in sent:
        one.wait_send()


def on_device(bands, iterate, forcing, start_state, damping, coriolis, coupling, edge_order):
    forward, inverse, lam = tables()
    flat = (C, T, Q * L)
    hbm = pl.BlockSpec(memory_space=pltpu.HBM)
    f32, i32 = jnp.float32, jnp.int32
    block = pltpu.VMEM((G, 4, 8, BLOCK), f32)
    staged = pltpu.VMEM((3, 8, Q * L), f32)
    own, pair = pltpu.VMEM((Q, 3, 8, L), f32), pltpu.VMEM((2, Q * L), i32)
    tiled = pltpu.VMEM((Q, C, T, L), f32)
    row = pltpu.VMEM((8, WIDE), f32)
    dma = pltpu.SemaphoreType.DMA
    out = pl.pallas_call(
        functools.partial(kernel, bands),
        out_shape=jax.ShapeDtypeStruct(flat, f32),
        in_specs=[hbm] * 10,
        out_specs=hbm,
        scratch_shapes=[
            pltpu.VMEM((T, T + 8), f32), pltpu.VMEM((T, T), f32), pltpu.VMEM((2, T, L), f32),
            tiled, tiled, tiled, staged, staged,
            own, pair, own, pair, own, pair, own,
            pltpu.VMEM((10, 8, WIDE), f32), row, row,
            pltpu.VMEM((EXT, 7, 8, Q * L), f32),
            pltpu.VMEM((EXT, 8, WIDE), f32),
            pltpu.VMEM((SWEEPS, EXT, 8, WIDE), f32),
            pltpu.VMEM((G, C, 8, L), f32),
        ]
        + [block] * 8
        + [dma((16,)), dma((10,)), dma((10,)), dma((7,)), dma((7,))]
        + [dma((7 * len(FORTH),))] * 4
        + [dma((7 * len(BACK),))] * 4,
        compiler_params=pltpu.CompilerParams(
            collective_id=0, has_side_effects=True, vmem_limit_bytes=60 * 1024 * 1024
        ),
    )(
        iterate.reshape(flat), forcing.reshape(flat), start_state, damping, coriolis, coupling,
        edge_order.reshape(2, Q * L), forward, inverse, lam,
    )
    return out.reshape(iterate.shape)


def solution(mesh):
    in_specs = (
        P(None, "tm", "mesh", None),
        P(None, "tm", "mesh", None),
        P(None, "mesh", None),
        P("mesh", None),
        P("mesh", None),
        P("mesh", None),
        P("mesh", None, None),
    )
    return jax.shard_map(
        functools.partial(on_device, mesh.shape["mesh"]),
        mesh=mesh, in_specs=in_specs, out_specs=P(None, "tm", "mesh", None), check_vma=False,
    )
```

time: 64.8 us -> 48.2 us (0.74)
  Pallas kernels: 55.4 us -> 46.3 us
  local copies, waits for them, and re-layouts: 8.73 us -> 1.77 us
    pallas_call x1, Pallas kernels: 55.4 us -> 46.3 us  [on_device(): pl.pallas_call(functools.partial(kernel, bands), out_shape=jax.ShapeDtype...]
    unnamed x21 -> x1, local copies, waits for them, and re-layouts: 8.73 us -> 1.77 us
where the time goes in v2:
time: 48.2 us; the launch traced here: 48 us
  Pallas kernels  46.3 us (96%)
  local copies, waits for them, and re-layouts  1.77 us (4%)
    pallas_call x1, Pallas kernels, on_device(): pl.pallas_call(functools.partial(kernel, bands), out_shape=jax.ShapeDtype...  46.3 us
    unnamed x1, local copies, waits for them, and re-layouts  1.77 us

profile of v2, /device:TPU:8, one launch (start us, length us, event | category | flops | bytes accessed | tf_op | source)
XLA Modules:
  0.0 48.0 jit_solution(3755031468383664160)
XLA Ops:
  0.0 46.3 %shard_map.100 = f32[3,64,512]{2,1,0:T(8,128)} custom-call(f32[3,64,512]{2,1,0:T(8,128)} %bitcast.5, f32[3,64,512]{2,1,0:T(8,128)} %bitcast.6, f32[3,8,512]{2,1,0:T(8,128)} %st_any.1, f32[8,512]{1,0:T(8,128)} %damp_any.1, f32[8,512]{1,0:T(8,128)} %cori_any.1, f32[8,512]{1,0:T(8,128)} %coup_any.1, s32[2,512]{1,0:T(2,128)} %bitcast.7, ...), custom_call_target="tpu_custom_call" | custom-call | tf_op jit(solution)/shard_map/pallas_call | solution.py:467
  46.3 1.8 %copy.12 = f32[3,8,8,512]{3,2,1,0:T(8,128)} copy(f32[3,8,8,512]{3,2,1,0:T(8,128)} %bitcast.4) | data formatting | bytes 786432

commit v3 on v2

--- a/solution.py
+++ b/solution.py
@@ -124,14 +124,14 @@
     above = lax.rem(band + 1, bands)
     peers = [lax.rem(me_x + dx, 4) * 2 + lax.rem(me_y + dy, 2) for dx, dy in FAR]
 
-    def by_lanes(wide_ref, tiled_ref, base, into):
-        pairs = [(wide_ref.at[:, :, pl.ds(q * L, L)], tiled_ref.at[q]) for q in range(Q)]
-        if not into:
-            pairs = [(b, a) for a, b in pairs]
-        return [pltpu.make_async_copy(a, b, in_sem.at[base + q]) for q, (a, b) in enumerate(pairs)]
-
-    fields = by_lanes(it_any, it_v, 0, True)
-    forces = by_lanes(fo_any, fo_v, 4, True)
+    def by_lanes(wide_ref, tiled_ref, base):
+        return [
+            pltpu.make_async_copy(wide_ref.at[:, :, pl.ds(q * L, L)], tiled_ref.at[q], in_sem.at[base + q])
+            for q in range(Q)
+        ]
+
+    fields = by_lanes(it_any, it_v, 0)
+    forces = by_lanes(fo_any, fo_v, 4)
     loads = [
         pltpu.make_async_copy(source, target, in_sem.at[8 + i])
         for i, (source, target) in enumerate(
@@ -444,11 +444,9 @@
                         out_v[q, c, pl.ds(r, 8, stride=8), :] = (
                             rows_t[r + 1, :, lanes(q, c)] + d_recv[2 * q + half, m, :, pl.ds(c * L, L)]
                         )
-    outs = by_lanes(out_ref, out_v, 0, False)
-    for one in outs:
-        one.start()
-    for one in outs:
-        one.wait()
+    for q in range(Q):
+        for c in range(C):
+            out_ref[c, :, pl.ds(q * L, L)] = out_v[q, c]
     for one in sent:
         one.wait_send()
 
@@ -466,9 +464,9 @@
     dma = pltpu.SemaphoreType.DMA
     out = pl.pallas_call(
         functools.partial(kernel, bands),
-        out_shape=jax.ShapeDtypeStruct(flat, f32),
+        out_shape=pltpu.VMEM(flat, f32),
         in_specs=[hbm] * 10,
-        out_specs=hbm,
+        out_specs=pl.BlockSpec(memory_space=pltpu.VMEM),
         scratch_shapes=[
             pltpu.VMEM((T, T + 8), f32), pltpu.VMEM((T, T), f32), pltpu.VMEM((2, T, L), f32),
             tiled, tiled, tiled, staged, staged,
@@ -484,11 +482,16 @@
         + [dma((7 * len(FORTH),))] * 4
         + [dma((7 * len(BACK),))] * 4,
         compiler_params=pltpu.CompilerParams(
-            collective_id=0, has_side_effects=True, vmem_limit_bytes=60 * 1024 * 1024
+            collective_id=0, has_side_effects=True, vmem_limit_bytes=40 * 1024 * 1024
         ),
     )(
-        iterate.reshape(flat), forcing.reshape(flat), start_state, damping, coriolis, coupling,
-        edge_order.reshape(2, Q * L), forward, inverse, lam,
+        *[
+            pltpu.with_memory_space_constraint(jnp.asarray(x), pltpu.HBM)
+            for x in (
+                iterate.reshape(flat), forcing.reshape(flat), start_state, damping, coriolis, coupling,
+                edge_order.reshape(2, Q * L), forward, inverse, lam,
+            )
+        ]
     )
     return out.reshape(iterate.shape)
 

time: 48.2 us -> 46.5 us (0.965)
  local copies, waits for them, and re-layouts: 1.77 us -> 0.75 us
  Pallas kernels: 46.3 us -> 45.6 us
    unnamed x1, local copies, waits for them, and re-layouts: 1.77 us -> 0.75 us
    pallas_call x1, Pallas kernels: 46.3 us -> 45.6 us  [on_device(): pl.pallas_call(functools.partial(kernel, bands), out_shape=pltpu.VMEM(fla...]
where the time goes in v3:
time: 46.5 us; the launch traced here: 46.3 us
  Pallas kernels  45.6 us (98%)
  local copies, waits for them, and re-layouts  0.75 us (2%)
    pallas_call x1, Pallas kernels, on_device(): pl.pallas_call(functools.partial(kernel, bands), out_shape=pltpu.VMEM(fla...  45.6 us

profile of v3, /device:TPU:8, one launch (start us, length us, event | category | flops | bytes accessed | tf_op | source)
XLA Modules:
  0.0 46.3 jit_solution(9121176379218856519)
XLA Ops:
  0.0 45.6 %shard_map.100 = f32[3,64,512]{2,1,0:T(8,128)S(1)} custom-call(f32[3,64,512]{2,1,0:T(8,128)} %bitcast.5, f32[3,64,512]{2,1,0:T(8,128)} %bitcast.6, f32[3,8,512]{2,1,0:T(8,128)} %st_any.1, f32[8,512]{1,0:T(8,128)} %damp_any.1, f32[8,512]{1,0:T(8,128)} %cori_any.1, f32[8,512]{1,0:T(8,128)} %coup_any.1, s32[2,512]{1,0:T(2,128)} %bitcast.7, ...), custom_call_target="tpu_custom_call" | custom-call | tf_op jit(solution)/shard_map/pallas_call | solution.py:465
  45.6 0.7 %copy.12 = f32[3,8,8,512]{3,2,1,0:T(8,128)} copy(f32[3,8,8,512]{3,2,1,0:T(8,128)S(1)} %bitcast.4) | data formatting | bytes 786432

commit v4 on v3

--- a/solution.py
+++ b/solution.py
@@ -24,6 +24,7 @@
 EXT = 18
 FORTH = ((0, 3), (3, 1))
 BACK = ((0, 1), (1, 2), (3, 1))
+UNROLL = True
 FAR = ((2, 1), (2, 0), (1, 1), (3, 1), (1, 0), (3, 0), (0, 1))
 
 
@@ -124,6 +125,12 @@
     above = lax.rem(band + 1, bands)
     peers = [lax.rem(me_x + dx, 4) * 2 + lax.rem(me_y + dy, 2) for dx, dy in FAR]
 
+    barrier = pltpu.get_barrier_semaphore()
+    for p in (below, above):
+        pl.semaphore_signal(barrier, 1, device_id={"mesh": p}, device_id_type=MESH)
+    for peer in peers:
+        pl.semaphore_signal(barrier, 1, device_id={"tm": peer}, device_id_type=MESH)
+
     def by_lanes(wide_ref, tiled_ref, base):
         return [
             pltpu.make_async_copy(wide_ref.at[:, :, pl.ds(q * L, L)], tiled_ref.at[q], in_sem.at[base + q])
@@ -141,14 +148,9 @@
             ]
         )
     ]
+
     for one in fields + forces + loads:
         one.start()
-    barrier = pltpu.get_barrier_semaphore()
-    for peer in peers:
-        pl.semaphore_signal(barrier, 1, device_id={"tm": peer}, device_id_type=MESH)
-    for p in (below, above):
-        pl.semaphore_signal(barrier, 1, device_id={"mesh": p}, device_id_type=MESH)
-
     sent = []
 
     def remote(src, dst, ss, rs, device):
@@ -161,16 +163,51 @@
     def side(index, src, dst, p):
         return remote(src, dst, side_send.at[index], side_recv.at[index], {"mesh": p})
 
-    def hop(src, dst, ss, rs, groups, index):
-        start, count = groups[index]
-        part = pl.ds(start, count)
-        return [
-            remote(
-                src.at[peer, part], dst.at[me, part],
-                ss.at[index * 7 + k], rs.at[index * 7 + k], {"tm": peer},
-            )
-            for k, peer in enumerate(peers)
-        ]
+    class Hop:
+        def __init__(self, src, dst, ss, rs, groups, index):
+            part, base = pl.ds(*groups[index]), index * G
+
+            def copy(peer):
+                return pltpu.make_async_remote_copy(
+                    src_ref=src.at[peer, part], dst_ref=dst.at[me, part],
+                    send_sem=ss.at[base + peer], recv_sem=rs.at[base + peer],
+                    device_id={"tm": peer}, device_id_type=MESH,
+                )
+
+            def out(peer):
+                return pltpu.make_async_remote_copy(
+                    src_ref=src.at[peer, part], dst_ref=dst.at[me, part],
+                    send_sem=ss.at[base + peer], recv_sem=rs.at[base + me],
+                    device_id={"tm": peer}, device_id_type=MESH,
+                )
+
+            self.copy, self.out = copy, out
+
+        def half(self, half, act):
+            for dx in (2, 1, 3):
+                act(lax.rem(me_x + dx, 4) * 2 + half)
+            pl.when(me_y != half)(lambda: act(me_x * 2 + half))
+
+        def start(self):
+            for peer in peers:
+                self.out(peer).start()
+
+        def arrive(self):
+            for peer in peers:
+                self.copy(peer).wait_recv()
+
+        def start_half(self, half):
+            self.half(half, lambda peer: self.out(peer).start())
+
+        def arrive_half(self, half):
+            self.half(half, lambda peer: self.copy(peer).wait_recv())
+
+        def sent(self):
+            for peer in peers:
+                self.copy(peer).wait_send()
+
+    def hops(src, dst, ss, rs, groups):
+        return [Hop(src, dst, ss, rs, groups, i) for i in range(len(groups))]
 
     def start(copies):
         for one in copies:
@@ -229,8 +266,8 @@
         for k, peer in enumerate(peers)
     ]
     start(hop_e)
-    hop_a = [hop(a_send, a_recv, a_ss, a_rs, FORTH, i) for i in range(len(FORTH))]
-    start(hop_a[0])
+    hop_a = hops(a_send, a_recv, a_ss, a_rs, FORTH)
+    hop_a[0].start()
     params = [
         side(2, own_c, high_c, below), side(3, own_c, low_c, above),
         side(4, own_o, high_o, below), side(5, own_o, low_o, above),
@@ -246,11 +283,14 @@
         tiles = [[ref[:, lanes(q, c)] for q in range(Q)] for c in range(C)]
         store(rows_t, row, [permuted(tiles[c], order(own_o, which)) for c in range(C)])
 
-    arrive(halos)
+    arrive(halos[:1])
+    halo(halo_hi, 9, 1)
+    residual_row(7, 1, 3)
+    hop_a[1].start_half(1)
+    arrive(halos[1:])
     halo(halo_lo, 0, 0)
-    halo(halo_hi, 9, 1)
-    residual_pair(3, 0)
-    start(hop_a[1])
+    residual_row(0, 0, 3)
+    hop_a[1].start_half(0)
     keep(a_send, a_recv, FORTH[1])
 
     lam_re = lam_ref[0, pl.ds(me * 8, 8), :]
@@ -300,12 +340,12 @@
         return e_recv.reshape(G * C * 8, L)[pl.ds(c * 8 + row, G, stride=C * 8), :]
 
     arrive(hop_e)
-    hop_b = [hop(b_send, b_recv, b_ss, b_rs, FORTH, i) for i in range(len(FORTH))]
+    hop_b = hops(b_send, b_recv, b_ss, b_rs, FORTH)
     for i, (begin, count) in enumerate(FORTH):
-        arrive(hop_a[i])
+        hop_a[i].arrive()
         for m in range(begin, begin + count):
             transform(fwd_ref[...], a_recv, b_send, m, previous(m))
-        start(hop_b[i])
+        hop_b[i].start()
         keep(b_send, b_recv, FORTH[i])
 
     arrive(params)
@@ -349,11 +389,15 @@
         tiles = load(src, source)
         store(src, to, [permuted(tiles[c], order(ref, which)) for c in range(C)])
 
+    def own_row(half, m):
+        r = 4 + m if half else 3 - m
+        for q in range(Q):
+            for c in range(C):
+                spec[MID + r, :, lanes(q, c)] = b_recv[2 * q + half, m, :, pl.ds(c * L, L)]
+
     def own_rows(m, _):
-        for half, r in ((0, 3 - m), (1, 4 + m)):
-            for q in range(Q):
-                for c in range(C):
-                    spec[MID + r, :, lanes(q, c)] = b_recv[2 * q + half, m, :, pl.ds(c * L, L)]
+        own_row(0, m)
+        own_row(1, m)
         return 0
 
     def own_first(m, _):
@@ -365,80 +409,100 @@
         return side(index, spec.at[pl.ds(src, count)], spec.at[pl.ds(dst, count)], p)
 
     rims = [
-        rim(6, MID + 1, HI + 1, 2, below), rim(7, MID + 5, LO, 2, above),
-        rim(8, MID, HI, 1, below), rim(9, MID + 7, LO + 2, 1, above),
+        rim(6, MID + 1, HI + 1, 2, below), rim(7, MID, HI, 1, below),
+        rim(8, MID + 5, LO, 2, above), rim(9, MID + 7, LO + 2, 1, above),
     ]
-    arrive(hop_b[0])
+    hop_b[0].arrive()
     lax.fori_loop(0, 3, own_rows, 0)
-    start(rims[:2])
+    start([rims[0], rims[2]])
     lax.fori_loop(0, 3, own_first, 0)
     lax.fori_loop(0, 2, sweep_pair(0, MID + 2, MID + 5), 0)
-    arrive(hop_b[1])
-    own_rows(3, 0)
-    start(rims[2:])
+    hop_b[1].arrive_half(1)
+    own_row(1, 3)
+    start(rims[3:])
+    hop_b[1].arrive_half(0)
+    own_row(0, 3)
+    start(rims[1:2])
     own_first(3, 0)
     ghost(0, LO + 3, MID, low_o, 1)
     ghost(0, HI - 1, MID + 7, high_o, 0)
     lax.fori_loop(0, 1, sweep_pair(0, MID + 1, MID + 6), 0)
     lax.fori_loop(0, 2, sweep_pair(1, MID + 2, MID + 5), 0)
 
-    hop_c = [hop(c_send, c_recv, c_ss, c_rs, BACK, i) for i in range(len(BACK))]
-
-    def last_pair(m):
-        for half, r in ((0, 3 - m), (1, 4 + m)):
-            tiles = sweep_row(2, MID + r)
-            for q in range(Q):
-                for c in range(C):
-                    c_send[2 * q + half, m, :, pl.ds(c * L, L)] = tiles[c][q]
-
-    def finish(i):
+    hop_c = hops(c_send, c_recv, c_ss, c_rs, BACK)
+
+    def last_row(half, m):
+        tiles = sweep_row(2, MID + (4 + m if half else 3 - m))
+        for q in range(Q):
+            for c in range(C):
+                c_send[2 * q + half, m, :, pl.ds(c * L, L)] = tiles[c][q]
+
+    def sweep_rows(level, first_one):
+        def body(i, _):
+            store(cur.at[level + 1], first_one + i, sweep_row(level, first_one + i))
+            return 0
+
+        lax.fori_loop(0, 2, body, 0, unroll=UNROLL)
+
+    def rim_first(first_one):
+        def body(i, _):
+            first_row(first_one + i)
+            return 0
+
+        lax.fori_loop(0, 3, body, 0)
+
+    def finish(half, i):
         begin, count = BACK[i]
-        if count == 1:
-            last_pair(begin)
-        else:
-            def body(m, _):
-                last_pair(m)
-                return 0
-
-            lax.fori_loop(begin, begin + count, body, 0)
-        start(hop_c[i])
-        keep(c_send, c_recv, BACK[i])
-
-    finish(0)
-    arrive(rims)
-
-    def rim_first(i, _):
-        first_row(LO + i)
-        first_row(HI + 2 - i)
-        return 0
-
-    lax.fori_loop(0, 3, rim_first, 0)
-    ghost(0, MID - 1, LO + 2, own_o, 0)
+
+        def body(m, _):
+            last_row(half, m)
+            return 0
+
+        lax.fori_loop(begin, begin + count, body, 0, unroll=UNROLL)
+        hop_c[i].start_half(half)
+
+    last_row(0, 0)
+    last_row(1, 0)
+    hop_c[0].start()
+    arrive(rims[:2])
+    rim_first(HI)
     ghost(0, MID + 8, HI, own_o, 1)
-    lax.fori_loop(0, 2, sweep_pair(0, LO + 1, HI + 1), 0)
-    lax.fori_loop(0, 1, sweep_pair(0, MID, MID + 7), 0)
-    ghost(1, LO + 3, MID, low_o, 1)
+    sweep_rows(0, HI)
+    store(cur.at[1], MID + 7, sweep_row(0, MID + 7))
     ghost(1, HI - 1, MID + 7, high_o, 0)
-    ghost(1, MID - 1, LO + 2, own_o, 0)
     ghost(1, MID + 8, HI, own_o, 1)
-    lax.fori_loop(0, 1, sweep_pair(1, LO + 2, HI), 0)
-    lax.fori_loop(0, 2, sweep_pair(1, MID, MID + 7), 0)
-    ghost(2, MID - 1, LO + 2, own_o, 0)
+    store(cur.at[2], HI, sweep_row(1, HI))
+    sweep_rows(1, MID + 6)
     ghost(2, MID + 8, HI, own_o, 1)
     for i in range(1, len(BACK)):
-        finish(i)
-
-    hop_d = [hop(d_send, d_recv, d_ss, d_rs, BACK, i) for i in range(len(BACK))]
+        finish(1, i)
+    arrive(rims[2:])
+    rim_first(LO)
+    ghost(0, MID - 1, LO + 2, own_o, 0)
+    sweep_rows(0, LO + 1)
+    store(cur.at[1], MID, sweep_row(0, MID))
+    ghost(1, LO + 3, MID, low_o, 1)
+    ghost(1, MID - 1, LO + 2, own_o, 0)
+    store(cur.at[2], LO + 2, sweep_row(1, LO + 2))
+    sweep_rows(1, MID)
+    ghost(2, MID - 1, LO + 2, own_o, 0)
+    for i in range(1, len(BACK)):
+        finish(0, i)
+    for group in BACK:
+        keep(c_send, c_recv, group)
+
+    hop_d = hops(d_send, d_recv, d_ss, d_rs, BACK)
     for i, (begin, count) in enumerate(BACK):
-        arrive(hop_c[i])
+        hop_c[i].arrive()
         for m in range(begin, begin + count):
             transform(inv_ref[...], c_recv, d_send, m, None)
-        start(hop_d[i])
+        hop_d[i].start()
         keep(d_send, d_recv, BACK[i])
-    for i, (begin, count) in enumerate(BACK):
-        arrive(hop_d[i])
-        for m in range(begin, begin + count):
-            for half, r in ((0, 3 - m), (1, 4 + m)):
+    for half in (1, 0):
+        for i, (begin, count) in enumerate(BACK):
+            hop_d[i].arrive_half(half)
+            for m in range(begin, begin + count):
+                r = 4 + m if half else 3 - m
                 for q in range(Q):
                     for c in range(C):
                         out_v[q, c, pl.ds(r, 8, stride=8), :] = (
@@ -449,6 +513,8 @@
             out_ref[c, :, pl.ds(q * L, L)] = out_v[q, c]
     for one in sent:
         one.wait_send()
+    for one in hop_a + hop_b + hop_c + hop_d:
+        one.sent()
 
 
 def on_device(bands, iterate, forcing, start_state, damping, coriolis, coupling, edge_order):
@@ -479,8 +545,8 @@
         ]
         + [block] * 8
         + [dma((16,)), dma((10,)), dma((10,)), dma((7,)), dma((7,))]
-        + [dma((7 * len(FORTH),))] * 4
-        + [dma((7 * len(BACK),))] * 4,
+        + [dma((G * len(FORTH),))] * 4
+        + [dma((G * len(BACK),))] * 4,
         compiler_params=pltpu.CompilerParams(
             collective_id=0, has_side_effects=True, vmem_limit_bytes=40 * 1024 * 1024
         ),

time: 46.5 us -> 44.1 us (0.948)
  Pallas kernels: 45.6 us -> 43.2 us
    pallas_call x1, Pallas kernels: 45.6 us -> 43.2 us  [on_device(): pl.pallas_call(functools.partial(kernel, bands), out_shape=pltpu.VMEM(fla...]
where the time goes in v4:
time: 44.1 us; the launch traced here: 43.9 us
  Pallas kernels  43.2 us (98%)
  local copies, waits for them, and re-layouts  0.75 us (2%)
    pallas_call x1, Pallas kernels, on_device(): pl.pallas_call(functools.partial(kernel, bands), out_shape=pltpu.VMEM(fla...  43.2 us

profile of v4, /device:TPU:8, one launch (start us, length us, event | category | flops | bytes accessed | tf_op | source)
XLA Modules:
  0.0 43.9 jit_solution(1388446804832638208)
XLA Ops:
  0.0 43.2 %shard_map.100 = f32[3,64,512]{2,1,0:T(8,128)S(1)} custom-call(f32[3,64,512]{2,1,0:T(8,128)} %bitcast.5, f32[3,64,512]{2,1,0:T(8,128)} %bitcast.6, f32[3,8,512]{2,1,0:T(8,128)} %st_any.1, f32[8,512]{1,0:T(8,128)} %damp_any.1, f32[8,512]{1,0:T(8,128)} %cori_any.1, f32[8,512]{1,0:T(8,128)} %coup_any.1, s32[2,512]{1,0:T(2,128)} %bitcast.7, ...), custom_call_target="tpu_custom_call" | custom-call | tf_op jit(solution)/shard_map/pallas_call | solution.py:531
  43.2 0.7 %copy.12 = f32[3,8,8,512]{3,2,1,0:T(8,128)} copy(f32[3,8,8,512]{3,2,1,0:T(8,128)S(1)} %bitcast.4) | data formatting | bytes 786432

commit v5 on v4

--- a/solution.py
+++ b/solution.py
@@ -22,7 +22,7 @@
 BLOCK = C * L
 LO, MID, HI = 0, 5, 15
 EXT = 18
-FORTH = ((0, 3), (3, 1))
+FORTH = ((1, 2), (0, 1), (3, 1))
 BACK = ((0, 1), (1, 2), (3, 1))
 UNROLL = True
 FAR = ((2, 1), (2, 0), (1, 1), (3, 1), (1, 0), (3, 0), (0, 1))
@@ -255,7 +255,8 @@
         residual_row(4 + m, 1, m)
         return 0
 
-    lax.fori_loop(0, 3, residual_pair, 0)
+    lax.fori_loop(1, 3, residual_pair, 0)
+    residual_pair(0, 0)
 
     pl.semaphore_wait(barrier, 9)
     halos = [side(0, rows_t.at[1], halo_hi, below), side(1, rows_t.at[8], halo_lo, above)]
@@ -268,6 +269,7 @@
     start(hop_e)
     hop_a = hops(a_send, a_recv, a_ss, a_rs, FORTH)
     hop_a[0].start()
+    hop_a[1].start()
     params = [
         side(2, own_c, high_c, below), side(3, own_c, low_c, above),
         side(4, own_o, high_o, below), side(5, own_o, low_o, above),
@@ -275,6 +277,7 @@
     start(params)
     e_recv[me] = it_v[me_x, :, last, :]
     keep(a_send, a_recv, FORTH[0])
+    keep(a_send, a_recv, FORTH[1])
 
     def order(ref, which):
         return [jnp.broadcast_to(ref[pl.ds(which, 1), pl.ds(q * L, L)], (8, L)) for q in range(Q)]
@@ -286,12 +289,12 @@
     arrive(halos[:1])
     halo(halo_hi, 9, 1)
     residual_row(7, 1, 3)
-    hop_a[1].start_half(1)
+    hop_a[2].start_half(1)
     arrive(halos[1:])
     halo(halo_lo, 0, 0)
     residual_row(0, 0, 3)
-    hop_a[1].start_half(0)
-    keep(a_send, a_recv, FORTH[1])
+    hop_a[2].start_half(0)
+    keep(a_send, a_recv, FORTH[2])
 
     lam_re = lam_ref[0, pl.ds(me * 8, 8), :]
     lam_im = lam_ref[1, pl.ds(me * 8, 8), :]
@@ -329,7 +332,7 @@
         if extra is not None:
             rows = jnp.concatenate([rows, extra], axis=0)
         dst[:, m] = jnp.dot(
-            table, rows, precision=lax.Precision.HIGHEST, preferred_element_type=jnp.float32
+            table, rows, precision=lax.Precision.HIGH, preferred_element_type=jnp.float32
         ).reshape(G, 8, BLOCK)
 
     def previous(m):
@@ -413,14 +416,17 @@
         rim(8, MID + 5, LO, 2, above), rim(9, MID + 7, LO + 2, 1, above),
     ]
     hop_b[0].arrive()
-    lax.fori_loop(0, 3, own_rows, 0)
+    lax.fori_loop(1, 3, own_rows, 0)
     start([rims[0], rims[2]])
-    lax.fori_loop(0, 3, own_first, 0)
+    lax.fori_loop(1, 3, own_first, 0)
+    hop_b[1].arrive()
+    own_rows(0, 0)
+    own_first(0, 0)
     lax.fori_loop(0, 2, sweep_pair(0, MID + 2, MID + 5), 0)
-    hop_b[1].arrive_half(1)
+    hop_b[2].arrive_half(1)
     own_row(1, 3)
     start(rims[3:])
-    hop_b[1].arrive_half(0)
+    hop_b[2].arrive_half(0)
     own_row(0, 3)
     start(rims[1:2])
     own_first(3, 0)
@@ -473,11 +479,14 @@
     ghost(1, MID + 8, HI, own_o, 1)
     store(cur.at[2], HI, sweep_row(1, HI))
     sweep_rows(1, MID + 6)
+    finish(1, 1)
     ghost(2, MID + 8, HI, own_o, 1)
-    for i in range(1, len(BACK)):
-        finish(1, i)
-    arrive(rims[2:])
-    rim_first(LO)
+    finish(1, 2)
+    arrive(rims[2:3])
+    first_row(LO)
+    first_row(LO + 1)
+    arrive(rims[3:])
+    first_row(LO + 2)
     ghost(0, MID - 1, LO + 2, own_o, 0)
     sweep_rows(0, LO + 1)
     store(cur.at[1], MID, sweep_row(0, MID))
@@ -485,12 +494,16 @@
     ghost(1, MID - 1, LO + 2, own_o, 0)
     store(cur.at[2], LO + 2, sweep_row(1, LO + 2))
     sweep_rows(1, MID)
+    finish(0, 1)
     ghost(2, MID - 1, LO + 2, own_o, 0)
-    for i in range(1, len(BACK)):
-        finish(0, i)
+    finish(0, 2)
     for group in BACK:
         keep(c_send, c_recv, group)
 
+    for one in sent:
+        one.wait_send()
+    for one in hop_a + hop_b:
+        one.sent()
     hop_d = hops(d_send, d_recv, d_ss, d_rs, BACK)
     for i, (begin, count) in enumerate(BACK):
         hop_c[i].arrive()
@@ -498,6 +511,8 @@
             transform(inv_ref[...], c_recv, d_send, m, None)
         hop_d[i].start()
         keep(d_send, d_recv, BACK[i])
+    for one in hop_c:
+        one.sent()
     for half in (1, 0):
         for i, (begin, count) in enumerate(BACK):
             hop_d[i].arrive_half(half)
@@ -511,9 +526,7 @@
     for q in range(Q):
         for c in range(C):
             out_ref[c, :, pl.ds(q * L, L)] = out_v[q, c]
-    for one in sent:
-        one.wait_send()
-    for one in hop_a + hop_b + hop_c + hop_d:
+    for one in hop_d:
         one.sent()
 
 

time: 44.1 us -> 43.5 us (0.986)
  Pallas kernels: 43.2 us -> 42.6 us
    pallas_call x1, Pallas kernels: 43.2 us -> 42.6 us  [on_device(): pl.pallas_call(functools.partial(kernel, bands), out_shape=pltpu.VMEM(fla...]
where the time goes in v5:
time: 43.5 us; the launch traced here: 43.4 us
  Pallas kernels  42.6 us (98%)
  local copies, waits for them, and re-layouts  0.75 us (2%)
    pallas_call x1, Pallas kernels, on_device(): pl.pallas_call(functools.partial(kernel, bands), out_shape=pltpu.VMEM(fla...  42.6 us

profile of v5, /device:TPU:8, one launch (start us, length us, event | category | flops | bytes accessed | tf_op | source)
XLA Modules:
  0.0 43.4 jit_solution(3449835085954577337)
XLA Ops:
  0.0 42.6 %shard_map.100 = f32[3,64,512]{2,1,0:T(8,128)S(1)} custom-call(f32[3,64,512]{2,1,0:T(8,128)} %bitcast.5, f32[3,64,512]{2,1,0:T(8,128)} %bitcast.6, f32[3,8,512]{2,1,0:T(8,128)} %st_any.1, f32[8,512]{1,0:T(8,128)} %damp_any.1, f32[8,512]{1,0:T(8,128)} %cori_any.1, f32[8,512]{1,0:T(8,128)} %coup_any.1, s32[2,512]{1,0:T(2,128)} %bitcast.7, ...), custom_call_target="tpu_custom_call" | custom-call | tf_op jit(solution)/shard_map/pallas_call | solution.py:544
  42.6 0.7 %copy.12 = f32[3,8,8,512]{3,2,1,0:T(8,128)} copy(f32[3,8,8,512]{3,2,1,0:T(8,128)S(1)} %bitcast.4) | data formatting | bytes 786432

commit v6 on v5

--- a/solution.py
+++ b/solution.py
@@ -23,9 +23,9 @@
 LO, MID, HI = 0, 5, 15
 EXT = 18
 FORTH = ((1, 2), (0, 1), (3, 1))
-BACK = ((0, 1), (1, 2), (3, 1))
+BACK = ((0, 1), (1, 1), (2, 2))
 UNROLL = True
-FAR = ((2, 1), (2, 0), (1, 1), (3, 1), (1, 0), (3, 0), (0, 1))
+FAR = ((2, 1), (1, 1), (3, 1), (2, 0), (1, 0), (3, 0), (0, 1))
 
 
 def tables():
@@ -133,7 +133,9 @@
 
     def by_lanes(wide_ref, tiled_ref, base):
         return [
-            pltpu.make_async_copy(wide_ref.at[:, :, pl.ds(q * L, L)], tiled_ref.at[q], in_sem.at[base + q])
+            pltpu.make_async_copy(
+                wide_ref.at[:, :, pl.ds(q * L, L)], tiled_ref.at[q, :, pl.ds(0, T), :], in_sem.at[base + q]
+            )
             for q in range(Q)
         ]
 
@@ -255,20 +257,20 @@
         residual_row(4 + m, 1, m)
         return 0
 
-    lax.fori_loop(1, 3, residual_pair, 0)
+    lax.fori_loop(1, 3, residual_pair, 0, unroll=UNROLL)
     residual_pair(0, 0)
 
     pl.semaphore_wait(barrier, 9)
     halos = [side(0, rows_t.at[1], halo_hi, below), side(1, rows_t.at[8], halo_lo, above)]
     start(halos)
     last = pl.ds(T - 8, 8)
+    hop_a = hops(a_send, a_recv, a_ss, a_rs, FORTH)
+    hop_a[0].start()
     hop_e = [
         remote(it_v.at[peer // 2, :, last, :], e_recv.at[me], e_ss.at[k], e_rs.at[k], {"tm": peer})
         for k, peer in enumerate(peers)
     ]
     start(hop_e)
-    hop_a = hops(a_send, a_recv, a_ss, a_rs, FORTH)
-    hop_a[0].start()
     hop_a[1].start()
     params = [
         side(2, own_c, high_c, below), side(3, own_c, low_c, above),
@@ -332,7 +334,7 @@
         if extra is not None:
             rows = jnp.concatenate([rows, extra], axis=0)
         dst[:, m] = jnp.dot(
-            table, rows, precision=lax.Precision.HIGH, preferred_element_type=jnp.float32
+            table, rows, precision=lax.Precision.HIGHEST, preferred_element_type=jnp.float32
         ).reshape(G, 8, BLOCK)
 
     def previous(m):
@@ -340,7 +342,7 @@
         return jnp.concatenate([e_flat(c, row) for c in range(C)], axis=1)
 
     def e_flat(c, row):
-        return e_recv.reshape(G * C * 8, L)[pl.ds(c * 8 + row, G, stride=C * 8), :]
+        return e_recv.reshape((G + 1) * C * 8, L)[pl.ds(c * 8 + row, G, stride=C * 8), :]
 
     arrive(hop_e)
     hop_b = hops(b_send, b_recv, b_ss, b_rs, FORTH)
@@ -416,13 +418,13 @@
         rim(8, MID + 5, LO, 2, above), rim(9, MID + 7, LO + 2, 1, above),
     ]
     hop_b[0].arrive()
-    lax.fori_loop(1, 3, own_rows, 0)
+    lax.fori_loop(1, 3, own_rows, 0, unroll=UNROLL)
     start([rims[0], rims[2]])
-    lax.fori_loop(1, 3, own_first, 0)
+    lax.fori_loop(1, 3, own_first, 0, unroll=UNROLL)
     hop_b[1].arrive()
     own_rows(0, 0)
     own_first(0, 0)
-    lax.fori_loop(0, 2, sweep_pair(0, MID + 2, MID + 5), 0)
+    lax.fori_loop(0, 2, sweep_pair(0, MID + 2, MID + 5), 0, unroll=UNROLL)
     hop_b[2].arrive_half(1)
     own_row(1, 3)
     start(rims[3:])
@@ -433,7 +435,7 @@
     ghost(0, LO + 3, MID, low_o, 1)
     ghost(0, HI - 1, MID + 7, high_o, 0)
     lax.fori_loop(0, 1, sweep_pair(0, MID + 1, MID + 6), 0)
-    lax.fori_loop(0, 2, sweep_pair(1, MID + 2, MID + 5), 0)
+    lax.fori_loop(0, 2, sweep_pair(1, MID + 2, MID + 5), 0, unroll=UNROLL)
 
     hop_c = hops(c_send, c_recv, c_ss, c_rs, BACK)
 
@@ -455,7 +457,7 @@
             first_row(first_one + i)
             return 0
 
-        lax.fori_loop(0, 3, body, 0)
+        lax.fori_loop(0, 3, body, 0, unroll=UNROLL)
 
     def finish(half, i):
         begin, count = BACK[i]
@@ -525,7 +527,7 @@
                         )
     for q in range(Q):
         for c in range(C):
-            out_ref[c, :, pl.ds(q * L, L)] = out_v[q, c]
+            out_ref[c, :, pl.ds(q * L, L)] = out_v[q, c, pl.ds(0, T), :]
     for one in hop_d:
         one.sent()
 
@@ -538,7 +540,7 @@
     block = pltpu.VMEM((G, 4, 8, BLOCK), f32)
     staged = pltpu.VMEM((3, 8, Q * L), f32)
     own, pair = pltpu.VMEM((Q, 3, 8, L), f32), pltpu.VMEM((2, Q * L), i32)
-    tiled = pltpu.VMEM((Q, C, T, L), f32)
+    tiled = pltpu.VMEM((Q, C, T + 8, L), f32)
     row = pltpu.VMEM((8, WIDE), f32)
     dma = pltpu.SemaphoreType.DMA
     out = pl.pallas_call(
@@ -554,7 +556,7 @@
             pltpu.VMEM((EXT, 7, 8, Q * L), f32),
             pltpu.VMEM((EXT, 8, WIDE), f32),
             pltpu.VMEM((SWEEPS, EXT, 8, WIDE), f32),
-            pltpu.VMEM((G, C, 8, L), f32),
+            pltpu.VMEM((G + 1, C, 8, L), f32),
         ]
         + [block] * 8
         + [dma((16,)), dma((10,)), dma((10,)), dma((7,)), dma((7,))]

time: 43.5 us -> 43.2 us (level)
  no operation moved by 1% of the time
where the time goes in v6:
time: 43.2 us; the launch traced here: 43.1 us
  Pallas kernels  42.3 us (98%)
  local copies, waits for them, and re-layouts  0.75 us (2%)
    pallas_call x1, Pallas kernels, on_device(): pl.pallas_call(functools.partial(kernel, bands), out_shape=pltpu.VMEM(fla...  42.3 us

profile of v6, /device:TPU:8, one launch (start us, length us, event | category | flops | bytes accessed | tf_op | source)
XLA Modules:
  0.0 43.1 jit_solution(9602861688796827902)
XLA Ops:
  0.0 42.3 %shard_map.100 = f32[3,64,512]{2,1,0:T(8,128)S(1)} custom-call(f32[3,64,512]{2,1,0:T(8,128)} %bitcast.5, f32[3,64,512]{2,1,0:T(8,128)} %bitcast.6, f32[3,8,512]{2,1,0:T(8,128)} %st_any.1, f32[8,512]{1,0:T(8,128)} %damp_any.1, f32[8,512]{1,0:T(8,128)} %cori_any.1, f32[8,512]{1,0:T(8,128)} %coup_any.1, s32[2,512]{1,0:T(2,128)} %bitcast.7, ...), custom_call_target="tpu_custom_call" | custom-call | tf_op jit(solution)/shard_map/pallas_call | solution.py:546
  42.3 0.7 %copy.12 = f32[3,8,8,512]{3,2,1,0:T(8,128)} copy(f32[3,8,8,512]{3,2,1,0:T(8,128)S(1)} %bitcast.4) | data formatting | bytes 786432

commit v7 on v6

--- a/solution.py
+++ b/solution.py
@@ -26,6 +26,15 @@
 BACK = ((0, 1), (1, 1), (2, 2))
 UNROLL = True
 FAR = ((2, 1), (1, 1), (3, 1), (2, 0), (1, 0), (3, 0), (0, 1))
+
+
+def split(table):
+    parts, rest = [], np.asarray(table, np.float32)
+    for _ in range(3):
+        parts.append(rest.astype(jnp.bfloat16))
+        rest = rest - parts[-1].astype(np.float32)
+    one, two, three = parts
+    return np.stack([np.concatenate([one, one, two], axis=1), np.concatenate([two, one, three], axis=1)])
 
 
 def tables():
@@ -50,10 +59,10 @@
                 inverse[:, row] = weight * wave / grow / T
                 lam[0, row] = 1.0 - beta * math.cos(2.0 * math.pi * freq / T)
                 lam[1, row] = 0.0 if slot == 0 else beta * math.sin(2.0 * math.pi * freq / T)
-    later = np.concatenate([forward[:, 8::8], np.zeros((T, 1))], axis=1)
+    later = np.concatenate([forward[:, 8::8], np.zeros((T, 9))], axis=1)
     forward = np.concatenate([forward, later], axis=1)
     lam = np.broadcast_to(lam[:, :, None], (2, T, L))
-    return [np.asarray(a, np.float32) for a in (forward, inverse, lam)]
+    return [split(forward), split(inverse), np.asarray(lam, np.float32)]
 
 
 def lanes(q, c):
@@ -332,10 +341,19 @@
     def transform(table, src, dst, m, extra):
         rows = src[:, m].reshape(T, BLOCK)
         if extra is not None:
-            rows = jnp.concatenate([rows, extra], axis=0)
-        dst[:, m] = jnp.dot(
-            table, rows, precision=lax.Precision.HIGHEST, preferred_element_type=jnp.float32
-        ).reshape(G, 8, BLOCK)
+            rows = jnp.concatenate([rows, extra, jnp.zeros((8, BLOCK), jnp.float32)], axis=0)
+        parts = []
+        for _ in range(3):
+            parts.append(rows.astype(jnp.bfloat16))
+            rows = rows - parts[-1].astype(jnp.float32)
+        one, two, three = parts
+        small = jnp.dot(
+            table[1], jnp.concatenate([two, three, one], axis=0), preferred_element_type=jnp.float32
+        )
+        large = jnp.dot(
+            table[0], jnp.concatenate([one, two, one], axis=0), preferred_element_type=jnp.float32
+        )
+        dst[:, m] = (large + small).reshape(G, 8, BLOCK)
 
     def previous(m):
         row = 3 - m + me_y * (1 + 2 * m)
@@ -349,7 +367,7 @@
     for i, (begin, count) in enumerate(FORTH):
         hop_a[i].arrive()
         for m in range(begin, begin + count):
-            transform(fwd_ref[...], a_recv, b_send, m, previous(m))
+            transform(fwd_ref, a_recv, b_send, m, previous(m))
         hop_b[i].start()
         keep(b_send, b_recv, FORTH[i])
 
@@ -510,7 +528,7 @@
     for i, (begin, count) in enumerate(BACK):
         hop_c[i].arrive()
         for m in range(begin, begin + count):
-            transform(inv_ref[...], c_recv, d_send, m, None)
+            transform(inv_ref, c_recv, d_send, m, None)
         hop_d[i].start()
         keep(d_send, d_recv, BACK[i])
     for one in hop_c:
@@ -549,7 +567,7 @@
         in_specs=[hbm] * 10,
         out_specs=pl.BlockSpec(memory_space=pltpu.VMEM),
         scratch_shapes=[
-            pltpu.VMEM((T, T + 8), f32), pltpu.VMEM((T, T), f32), pltpu.VMEM((2, T, L), f32),
+            pltpu.VMEM((2, T, 3 * (T + 16)), jnp.bfloat16), pltpu.VMEM((2, T, 3 * T), jnp.bfloat16), pltpu.VMEM((2, T, L), f32),
             tiled, tiled, tiled, staged, staged,
             own, pair, own, pair, own, pair, own,
             pltpu.VMEM((10, 8, WIDE), f32), row, row,

time: 43.2 us -> 43.4 us (level)
  no operation moved by 1% of the time
where the time goes in v7:
time: 43.4 us; the launch traced here: 43.2 us
  Pallas kernels  42.5 us (98%)
  local copies, waits for them, and re-layouts  0.75 us (2%)
    pallas_call x1, Pallas kernels, on_device(): pl.pallas_call(functools.partial(kernel, bands), out_shape=pltpu.VMEM(fla...  42.5 us

profile of v7, /device:TPU:8, one launch (start us, length us, event | category | flops | bytes accessed | tf_op | source)
XLA Modules:
  0.0 43.2 jit_solution(9786784189174827219)
XLA Ops:
  0.0 42.5 %shard_map.100 = f32[3,64,512]{2,1,0:T(8,128)S(1)} custom-call(f32[3,64,512]{2,1,0:T(8,128)} %bitcast.5, f32[3,64,512]{2,1,0:T(8,128)} %bitcast.6, f32[3,8,512]{2,1,0:T(8,128)} %st_any.1, f32[8,512]{1,0:T(8,128)} %damp_any.1, f32[8,512]{1,0:T(8,128)} %cori_any.1, f32[8,512]{1,0:T(8,128)} %coup_any.1, s32[2,512]{1,0:T(2,128)} %bitcast.7, ...), custom_call_target="tpu_custom_call" | custom-call | tf_op jit(solution)/shard_map/pallas_call | solution.py:564
  42.5 0.7 %copy.12 = f32[3,8,8,512]{3,2,1,0:T(8,128)} copy(f32[3,8,8,512]{3,2,1,0:T(8,128)S(1)} %bitcast.4) | data formatting | bytes 786432
